TPU v7x, 512 devices: a whole 4x4x16 slice. The times are simulated.
512 devices in a mesh: lat: 16 (over x, z_hi, core), lon: 32 (over y, z_lo).
Axes of the slice: x: 4, y: 4, z: 16 (z_hi: 2, z_lo: 8; z = z_hi * 8 + z_lo), core: 2. Of those that a mesh axis runs over, the one named last changes fastest.
Arguments:
- field: float32 [2, 192, 384, 384], P(None, 'lat', 'lon'), may hold values from -6 to 6
- norm_gain: float32 [2, 384], replicated, may hold values from 0.5 to 1.5
- norm_bias: float32 [2, 384], replicated, may hold values from -3 to 3
- qkv_weight: bfloat16 [2, 384, 1152], replicated, may hold values from -3.7 to 3.7
- qkv_bias: float32 [2, 1152], replicated, may hold values from -2 to 2
- proj_weight: bfloat16 [2, 384, 384], replicated, may hold values from -0.3125 to 0.3125
- proj_bias: float32 [2, 384], replicated, may hold values from -2 to 2
- earth_bias: bfloat16 [2, 16, 12, 6336], P(None, 'lat'), may hold values from -4 to 4
Outputs:
- mixed: float32 [2, 192, 384, 384], P(None, 'lat', 'lon')
All inputs are finite; a program needn't handle non-finite values.
Results may differ from a plain program's by a relative error of at most 0.012.
The roundings to bfloat16 on the way count: a program that leaves them out, or rounds other values in their place, can miss the bound.
Values may be sent and summed in bfloat16 or wider, within the bound.
No kernel may reach another device: no remote copies, remote signals or barrier semaphores. Data moves between devices by JAX's collectives and lax.ppermute only.
A program may use at most 128 MiB of HBM per device.

v0:
```python
import functools

import jax
import jax.numpy as jnp
import numpy as np
from jax import lax
from jax.experimental import pallas as pl
from jax.experimental.pallas import tpu as pltpu
from jax.sharding import PartitionSpec as P

Z = 2
WH = 12
WW = 6
HALF = WH // 2
SPAN = 2 * WW - 1
CELLS = WW * Z * HALF
TOKENS = 2 * CELLS
SIDE = CELLS // 2
GROUP = Z * WH
LANES = 128
PAD = 256
PACKED = 3 * LANES
LINE = WH * SPAN
LOG2E = float(np.log2(np.e))
VMEM_LIMIT = 60 * 1024 * 1024


def grid_of(*sizes):
    return [part.reshape(-1) for part in np.meshgrid(*map(np.arange, sizes), indexing="ij")]


def one_hot(rows, columns, width):
    table = np.zeros((len(rows), width), np.float32)
    keep = columns >= 0
    table[np.arange(len(rows))[keep], columns[keep]] = 1.0
    return table


def packed_lane(level, entry):
    lane = (entry + LANES - 2) % PAD
    tail = 2 * LANES + (lane + 64 * level) % LANES
    return np.where(lane >= LANES, level * LANES + lane - LANES, tail)


def lane_selector():
    half, col, level, row = grid_of(2, WW, Z, HALF)
    row = row + half * HALF
    table = np.zeros((PACKED, WW, PAD), np.float32)
    for w in range(WW):
        entry = row * SPAN + w - col + WW - 1
        table[packed_lane(level, entry), w, np.arange(TOKENS)] = 1.0
    return table.reshape(PACKED, WW * PAD)


def full_rows():
    half, col, level, row = grid_of(2, WW, Z, HALF)
    place = col * GROUP + level * WH + half * HALF + row
    return one_hot(place, place, TOKENS)


def table_rows():
    position = np.concatenate([31 - np.arange(32), 47 - np.arange(16)])
    picks = []
    for block in range(2):
        for key_level in range(Z):
            level, row = grid_of(Z, WH)
            picks.append(2 * position[(level * Z + key_level) * WH + row] + block)
    picks = np.concatenate(picks)
    return one_hot(picks, picks, 96)


def native_to_windows(windows):
    window, half, col, level, row = grid_of(windows, 2, WW, Z, HALF)
    place = ((half * HALF + row) * windows * WW + window * WW + col) * Z + level
    return one_hot(place, place, len(place))


def windows_to_native(windows):
    return native_to_windows(windows).T


def strip_from_native(cols):
    half, col, level, row = grid_of(2, cols + WW, Z, HALF)
    own = col - WW // 2
    place = ((half * HALF + row) * cols + own) * Z + level
    place = np.where((own >= 0) & (own < cols), place, -1)
    return one_hot(place, place, WH * cols * Z)


def strip_from_sides(cols):
    half, col, level, row = grid_of(2, cols + WW, Z, HALF)
    own = col - WW // 2
    inside = np.where(own < 0, own + WW, own - cols)
    place = ((half * WW + inside) * Z + level) * HALF + row
    place = np.where((own >= 0) & (own < cols), -1, place)
    return one_hot(place, place, TOKENS)


def native_from_queries():
    row, col, level = grid_of(HALF, 2 * WW, Z)
    middle = (col >= 3) & (col < 9)
    column = np.where(middle, col - 3, np.where(col < 3, col + 3, col - 9))
    place = ((np.where(middle, 0, 1) * WW + column) * Z + level) * HALF + row
    return one_hot(place, place, TOKENS)


def const(table):
    return jnp.asarray(table, jnp.bfloat16)


def exact(table, rows):
    return jnp.dot(table, rows, preferred_element_type=jnp.float32)


def normalized(grid, gain, offset):
    center = grid - jnp.mean(grid, axis=-1, keepdims=True)
    spread = jnp.mean(center * center, axis=-1, keepdims=True)
    return (center * lax.rsqrt(spread + 1e-05) * gain + offset).astype(jnp.bfloat16)


def pack_lines(near, far):
    lane = lax.broadcasted_iota(jnp.int32, near[:, LANES:].shape, 1)
    other = (lane >= 32) & (lane < 96)
    tail = jnp.where(other, pltpu.roll(far[:, :LANES], 64, 1), near[:, :LANES])
    return jnp.concatenate([near[:, LANES:], far[:, LANES:], tail], axis=1)


def table_kernel(raw_ref, pick_ref, first_ref, second_ref, lines):
    heads = raw_ref.shape[0]
    length = raw_ref.shape[2]
    tiles = -(-length // LANES)
    lines[:, 64:96, LANES:] = jnp.zeros((heads, 32, LANES), jnp.float32)
    for tile in range(tiles):
        size = min(LANES, length - tile * LANES)
        block = raw_ref[:, :, tile * LANES : tile * LANES + size].astype(jnp.float32)
        for line in (tile, tile - 1):
            side = (tile - line) * LANES
            if line < 0:
                continue
            if line < 32:
                place = 31 - line
                lines[:, 2 * place : 2 * place + 2, side : side + size] = block
            if line >= 33:
                place = 47 - (line - 33)
                if place >= 32:
                    lines[:, 2 * place : 2 * place + 2, side : side + size] = block
    for head in range(heads):
        rolled = jnp.concatenate(
            [
                pltpu.roll(lines[head, :64], 0, 1, stride=2, stride_axis=0),
                pltpu.roll(lines[head, 64:], 64, 1, stride=2, stride_axis=0),
            ],
            axis=0,
        ).astype(jnp.bfloat16)
        rows = exact(pick_ref[...], rolled)
        first = pltpu.roll(rows[:48], 2, 1)
        at = slice(head * GROUP, (head + 1) * GROUP)
        first_ref[at] = pack_lines(first[:24], first[24:]).astype(jnp.bfloat16)
        second_ref[at] = pack_lines(rows[48:72], rows[72:]).astype(jnp.bfloat16)


def dense_groups(table, lanes, rows, groups):
    spread = exact(table, lanes)
    for group in range(groups):
        part = spread[group * GROUP : (group + 1) * GROUP]
        stacked = jnp.concatenate(
            [part[:, w * PAD : w * PAD + TOKENS] for w in range(WW)], axis=0
        ).astype(jnp.bfloat16)
        yield group, exact(rows, stacked)


def attend(packed, bias, heads):
    rows, width = packed.shape[0], packed.shape[1] // 3
    head_dim = width // heads
    per_tile = LANES // head_dim
    lane = lax.broadcasted_iota(jnp.int32, (rows, LANES), 1) // head_dim
    ones = jnp.ones((rows, LANES), jnp.bfloat16)
    tiles = []
    for start in range(0, width, LANES):
        query, keys, values = (
            packed[:, start + i * width : start + i * width + LANES] for i in range(3)
        )
        values = jnp.concatenate([values, ones], axis=1)
        total = jnp.zeros((rows, LANES), jnp.float32)
        for part in range(per_tile):
            mine = lane == part
            chosen = jnp.where(mine, query, jnp.zeros_like(query))
            scores = lax.dot_general(
                chosen, keys, (((1,), (1,)), ((), ())), preferred_element_type=jnp.float32
            )
            scores = scores * (LOG2E * head_dim ** (-0.5)) + bias(start // head_dim + part)
            top = jnp.max(scores, axis=-1, keepdims=True)
            weights = jnp.exp2(scores - top).astype(jnp.bfloat16)
            mixed = jnp.dot(weights, values, preferred_element_type=jnp.float32)
            total = jnp.where(mine, mixed[:, :LANES] / mixed[:, LANES:], total)
        tiles.append(total)
    return jnp.concatenate(tiles, axis=1)


def inner_columns(rows, width):
    index = lax.broadcasted_iota(jnp.int32, (rows, width), 0)
    return index - jnp.where(index >= CELLS, CELLS, 0) < SIDE


def first_kernel(
    heads, field_ref, gain_ref, offset_ref, qkv_w, qkv_b, proj_w, proj_b, table_ref, lanes_ref,
    rows_ref, order_ref, back_ref, first_ref, second_ref, bias_ref, core_ref,
):
    for head, dense in dense_groups(table_ref[...], lanes_ref[...], rows_ref[...], heads):
        bias_ref[head] = dense * LOG2E
    cells, depth, width = field_ref.shape
    grid = field_ref[...].reshape(cells * depth, width)
    tokens = normalized(grid, gain_ref[0:1], offset_ref[0:1])
    tokens = exact(order_ref[...], tokens).astype(jnp.bfloat16)
    packed = jnp.dot(tokens, qkv_w[...], preferred_element_type=jnp.float32) + qkv_b[0:1]
    packed = packed.astype(jnp.bfloat16)
    for window in range(2):
        at = slice(window * TOKENS, (window + 1) * TOKENS)
        core_ref[at] = attend(packed[at], bias_ref.__getitem__, heads)
    core = exact(back_ref[...], core_ref[...].astype(jnp.bfloat16)).astype(jnp.bfloat16)
    result = jnp.dot(core, proj_w[...], preferred_element_type=jnp.float32) + proj_b[0:1]
    first = grid + result
    first_ref[...] = first
    second_ref[...] = normalized(first, gain_ref[1:2], offset_ref[1:2])


def edge_kernel(
    heads, place_ref, second_ref, near_ref, wrap_ref, gain_ref, offset_ref, qkv_w, qkv_b, proj_w,
    proj_b, bias_ref, side_ref, strip_ref, edge_ref, send_ref, keep_ref, core_ref,
):
    width = second_ref.shape[1]
    near = near_ref[...].astype(jnp.float32).reshape(TOKENS, width)
    wrap = wrap_ref[...].astype(jnp.float32).reshape(TOKENS, width)
    odd = place_ref[1] == 1
    left = exact(side_ref[...], jnp.where(odd, near, wrap).astype(jnp.bfloat16))
    right = exact(side_ref[...], jnp.where(odd, wrap, near).astype(jnp.bfloat16))
    tokens = normalized(jnp.concatenate([left, right], axis=0), gain_ref[0:1], offset_ref[0:1])
    packed = jnp.dot(tokens, qkv_w[...], preferred_element_type=jnp.float32) + qkv_b[0:1]
    packed = packed.astype(jnp.bfloat16)
    for window in range(2):
        at = slice(window * TOKENS, (window + 1) * TOKENS)
        core_ref[at] = attend(packed[at], bias_ref.__getitem__, heads)
    inner = inner_columns(TOKENS, width)
    core = jnp.where(inner, core_ref[TOKENS:], core_ref[:TOKENS]).astype(jnp.bfloat16)
    result = jnp.dot(core, proj_w[...], preferred_element_type=jnp.float32) + proj_b[0:1]
    edge = jnp.where(inner, right, left) + result
    edge = normalized(edge, gain_ref[1:2], offset_ref[1:2])
    strip = exact(strip_ref[...], second_ref[...]) + exact(edge_ref[...], edge)
    half = strip.shape[0] // 2
    send_ref[...] = strip[:half].astype(jnp.bfloat16)
    keep_ref[...] = strip[half:].astype(jnp.bfloat16)


def bias_kernel(heads, flag_ref, table_ref, lanes_ref, rows_ref, out_ref):
    upper = lax.broadcasted_iota(jnp.int32, (TOKENS, TOKENS), 0) < CELLS
    left = lax.broadcasted_iota(jnp.int32, (TOKENS, TOKENS), 1) < CELLS
    barred = jnp.where(upper != left, flag_ref[0] * -1000000000.0, 0.0)
    for head, dense in dense_groups(table_ref[...], lanes_ref[...], rows_ref[...], heads):
        out_ref[head] = (dense + barred) * LOG2E


def second_kernel(
    heads, own_ref, got_ref, qkv_w, qkv_b, proj_w, proj_b, bias_ref, back_ref, keep_ref, send_ref,
    core_ref,
):
    width = own_ref.shape[1]
    own, got = own_ref[...].astype(jnp.float32), got_ref[...].astype(jnp.float32)
    tokens = []
    for window in range(3):
        at = slice(window * CELLS, (window + 1) * CELLS)
        tokens += [own[at], got[at]]
    tokens = jnp.concatenate(tokens, axis=0).astype(jnp.bfloat16)
    packed = jnp.dot(tokens, qkv_w[...], preferred_element_type=jnp.float32) + qkv_b[1:2]
    packed = packed.astype(jnp.bfloat16)
    for window in range(3):
        at = slice(window * TOKENS, (window + 1) * TOKENS)
        core_ref[window] = attend(packed[at], bias_ref.__getitem__, heads)
    inner = inner_columns(CELLS, width)
    for start, out_ref in ((CELLS, send_ref), (0, keep_ref)):
        at = slice(start, start + CELLS)
        outer = jnp.where(inner, core_ref[2, at], core_ref[0, at])
        core = jnp.concatenate([core_ref[1, at], outer], axis=0).astype(jnp.bfloat16)
        core = exact(back_ref[...], core).astype(jnp.bfloat16)
        result = jnp.dot(core, proj_w[...], preferred_element_type=jnp.float32) + proj_b[1:2]
        out_ref[...] = result.astype(out_ref.dtype)


def final_kernel(first_ref, keep_ref, got_ref, out_ref):
    got = got_ref[...].astype(jnp.float32)
    result = first_ref[...] + jnp.concatenate([got, keep_ref[...]], axis=0)
    out_ref[...] = result.reshape(out_ref.shape)


def exchanged(block, near):
    count = lax.axis_size("lon")
    partner = [i ^ 1 if near else (i + (1 if i % 2 else -1)) % count for i in range(count)]
    return lax.ppermute(block, "lon", [(i, partner[i]) for i in range(count)])


def passed_along(block, axis, distance):
    count = lax.axis_size(axis)
    return lax.ppermute(block, axis, [((i - distance) % count, i) for i in range(count)])


VMEM = pl.BlockSpec(memory_space=pltpu.VMEM)
SMEM = pl.BlockSpec(memory_space=pltpu.SMEM)
WHOLE = lambda shape: pl.BlockSpec(shape, lambda i: (0,) * len(shape))


def chosen(array, which):
    size = array.shape[1:]
    return pl.BlockSpec((None, *size), lambda i: (which,) + (0,) * len(size))


def run(kernel, name, operands, specs, outs, scratch=(), flops=10**9):
    specs = [WHOLE(x.shape) if s is None else s for x, s in zip(operands, specs, strict=True)]
    return pl.pallas_call(
        kernel,
        grid=(1,),
        out_shape=[jax.ShapeDtypeStruct(*out) for out in outs],
        in_specs=specs,
        out_specs=[WHOLE(shape) for shape, _ in outs],
        scratch_shapes=list(scratch),
        compiler_params=pltpu.CompilerParams(vmem_limit_bytes=VMEM_LIMIT),
        cost_estimate=pl.CostEstimate(flops=flops, bytes_accessed=4000000, transcendentals=0),
        name=name,
    )(*operands)


def per_device(
    field, norm_gain, norm_bias, qkv_weight, qkv_bias, proj_weight, proj_bias, earth_bias
):
    depth, lat_rows, lon_cols, width = field.shape
    heads = earth_bias.shape[2]
    f32, bf16 = jnp.float32, jnp.bfloat16
    lat, lon = lax.axis_index("lat"), lax.axis_index("lon")
    place = jnp.stack([lat % 2, lon % 2]).astype(jnp.int32)
    last = (lat == lax.axis_size("lat") - 1).astype(f32).reshape(1)
    native = jnp.transpose(field, (1, 2, 0, 3))
    raw = jnp.transpose(earth_bias[:, 0], (1, 0, 2))

    halves = native.astype(bf16)
    odd = place[1] == 1
    to_wrap = jnp.where(odd, halves[:, WW:], halves[:, :WW])
    to_near = jnp.where(odd, halves[:, :WW], halves[:, WW:])
    wrap = exchanged(to_wrap, False)
    near = exchanged(to_near, True)

    rows = heads * WH
    lanes = const(lane_selector())
    table0, table1 = run(
        table_kernel,
        "tables",
        (raw, const(table_rows())),
        (None, None),
        [((2 * rows, PACKED), bf16)] * 2,
        [pltpu.VMEM((heads, 96, PAD), f32)],
    )
    strip = (lon_cols + WW) * Z * HALF
    cells = lat_rows * lon_cols
    first, second, bias0 = run(
        functools.partial(first_kernel, heads),
        "first_block",
        (
            native.reshape(cells, depth, width), norm_gain, norm_bias, qkv_weight, qkv_bias,
            proj_weight, proj_bias, table0, lanes, const(full_rows()),
            const(native_to_windows(2)), const(windows_to_native(2)),
        ),
        (None, None, None, chosen(qkv_weight, 0), None, chosen(proj_weight, 0)) + (None,) * 6,
        [((cells * depth, width), f32), ((cells * depth, width), bf16), ((heads, TOKENS, TOKENS), f32)],
        [pltpu.VMEM((2 * TOKENS, width), f32)],
    )
    send, keep = run(
        functools.partial(edge_kernel, heads),
        "first_block_edges",
        (
            place, second, near.reshape(cells // 2, depth, width),
            wrap.reshape(cells // 2, depth, width), norm_gain, norm_bias, qkv_weight, qkv_bias,
            proj_weight, proj_bias, bias0, const(native_to_windows(1)),
            const(strip_from_native(lon_cols)), const(strip_from_sides(lon_cols)),
        ),
        (SMEM, None, None, None, None, None, chosen(qkv_weight, 0), None, chosen(proj_weight, 0))
        + (None,) * 5,
        [((strip, width), bf16), ((strip, width), bf16)],
        [pltpu.VMEM((2 * TOKENS, width), f32)],
    )
    from_above = passed_along(send, "lat", -1)
    (bias1,) = run(
        functools.partial(bias_kernel, heads),
        "second_bias",
        (last, table1, lanes, const(full_rows())),
        (SMEM, None, None, None),
        [((heads, TOKENS, TOKENS), f32)],
    )
    kept, leaving = run(
        functools.partial(second_kernel, heads),
        "second_block",
        (
            keep, from_above, qkv_weight, qkv_bias, proj_weight, proj_bias, bias1,
            const(native_from_queries()),
        ),
        (None, None, chosen(qkv_weight, 1), None, chosen(proj_weight, 1)) + (None,) * 3,
        [((TOKENS, width), f32), ((TOKENS, width), bf16)],
        [pltpu.VMEM((3, TOKENS, width), f32)],
    )
    from_below = passed_along(leaving, "lat", 1)
    (mixed,) = run(
        final_kernel,
        "final_sum",
        (first, kept, from_below),
        (None,) * 3,
        [((cells, depth, width), f32)],
    )
    return jnp.transpose(mixed.reshape(lat_rows, lon_cols, depth, width), (2, 0, 1, 3))


def solution(mesh):
    in_specs = (P(None, "lat", "lon", None), P(), P(), P(), P(), P(), P(), P(None, "lat", None, None))
    out_specs = P(None, "lat", "lon", None)
    return jax.shard_map(
        per_device, mesh=mesh, in_specs=in_specs, out_specs=out_specs, check_vma=False
    )
```

profile of v0, /device:TPU:32, one launch (start us, length us, event | category | flops | bytes accessed | tf_op | source)
XLA Modules:
  0.0 74.3 jit_solution(686417915336137770)
XLA Ops:
  0.0 1.2 %bitcast_convert_fusion = bf16[12,12,2,384]{3,2,1,0:T(2,128)(2,1)S(1)} fusion(f32[2,12,12,384]{3,0,2,1:T(2,128)} %param.18), kind=kLoop, calls=%fused_computation | loop fusion | flops 110592 | bytes 663552 | tf_op jit(solution)/shard_map/convert_element_type | solution.py:342
  1.2 0.2 broadcast_select_fusion
  1.4 7.4 %collective-permute-start = (bf16[12,6,2,384]{3,2,1,0:T(2,128)(2,1)S(1)}, bf16[12,6,2,384]{3,2,1,0:T(2,128)(2,1)S(1)}, u32[]{:S(2)}, u32[]{:S(2)}) collective-permute-start(bf16[12,6,2,384]{3,2,1,0:T(2,128)(2,1)S(1)} %get-tuple-element.24), channel_id=1, source_target_pairs={{0,1},{1,0},{2,3},{3,2},{4,5},{5,4},{6,7},{7,6},{8,9},{9,8},{10,11... | collective-permute-start | bytes 331784 | tf_op jit(solution)/shard_map/ppermute | solution.py:297
  8.8 1.9 %collective-permute-start.1 = (bf16[12,6,2,384]{3,2,1,0:T(2,128)(2,1)S(1)}, bf16[12,6,2,384]{3,2,1,0:T(2,128)(2,1)S(1)}, u32[]{:S(2)}, u32[]{:S(2)}) collective-permute-start(bf16[12,6,2,384]{3,2,1,0:T(2,128)(2,1)S(1)} %get-tuple-element.23), channel_id=1, source_target_pairs={{0,31},{1,2},{2,1},{3,4},{4,3},{5,6},{6,5},{7,8},{8,7},{9,10},{10,... | collective-permute-start | bytes 331784 | tf_op jit(solution)/shard_map/ppermute | solution.py:297
  10.7 2.6 %tables.1 = (bf16[288,384]{1,0:T(8,128)(2,1)}, bf16[288,384]{1,0:T(8,128)(2,1)}) custom-call(bf16[12,2,6336]{2,1,0:T(2,128)(2,1)} %bitcast.18, bf16[96,96]{1,0:T(8,128)(2,1)} %constant.48.clone.pick_ref), custom_call_target="tpu_custom_call" | custom-call | flops 1000000000 | bytes 4000000 | tf_op jit(solution)/shard_map/tables/pallas_call | solution.py:317
  13.3 6.8 %first_block.1 = (f32[288,384]{1,0:T(8,128)}, bf16[288,384]{1,0:T(8,128)(2,1)}, f32[12,144,144]{2,1,0:T(8,128)}) custom-call(f32[144,2,384]{2,1,0:T(2,128)} %bitcast.15, f32[2,384]{1,0:T(2,128)} %gain_ref.3, f32[2,384]{1,0:T(2,128)} %offset_ref.3, bf16[2,384,1152]{2,1,0:T(8,128)(2,1)} %qkv_w.5, f32[2,1152]{1,0:T(2,128)} %qkv_b.5, ...), custom_call_target="tpu_custom_call" | custom-call | flops 1000000000 | bytes 4000000 | tf_op jit(solution)/shard_map/first_block/pallas_call | solution.py:317
  20.1 0.6 pad_add_fusion.place_ref
  20.7 0.0 collective-permute-done
  20.7 0.0 copy-start.1
  20.7 0.0 collective-permute-done.1
  20.7 0.0 copy-start.2
  20.7 0.6 copy-done.1
  21.4 0.0 copy-done.2
  21.4 5.7 %first_block_edges.1 = (bf16[216,384]{1,0:T(8,128)(2,1)}, bf16[216,384]{1,0:T(8,128)(2,1)}) custom-call(s32[2]{0:T(128)} %pad_add_fusion.place_ref, bf16[288,384]{1,0:T(8,128)(2,1)} %get-tuple-element.16.second_ref, bf16[72,2,384]{2,1,0:T(2,128)(2,1)} %bitcast.16, bf16[72,2,384]{2,1,0:T(2,128)(2,1)} %bitcast.17, f32[2,384]{1,0:T(2,128)} %gain_ref.3, ...), custom_call_target="tpu_custom_call" | custom-call | flops 1000000000 | bytes 4000000 | tf_op jit(solution)/shard_map/first_block_edges/pallas_call | solution.py:317
  27.1 12.4 %collective-permute-start.2 = (bf16[216,384]{1,0:T(8,128)(2,1)}, bf16[216,384]{1,0:T(8,128)(2,1)S(1)}, u32[]{:S(2)}, u32[]{:S(2)}) collective-permute-start(bf16[216,384]{1,0:T(8,128)(2,1)} %get-tuple-element.19), channel_id=1, source_target_pairs={{32,0},{64,32},{96,64},{128,96},{160,128},{192,160},{224,192},{256... | collective-permute-start | bytes 497672 | tf_op jit(solution)/shard_map/ppermute | solution.py:302
  39.5 3.5 %second_bias.1.bias_ref = f32[12,144,144]{2,1,0:T(8,128)} custom-call(f32[1]{0:T(128)} %bitcast.8.flag_ref, bf16[288,384]{1,0:T(8,128)(2,1)} %get-tuple-element.20.table_ref, bf16[384,1536]{1,0:T(8,128)(2,1)} %constant.47.clone.lanes_ref, bf16[144,144]{1,0:T(8,128)(2,1)} %constant.49.clone.rows_ref), custom_call_target="tpu_custom_call" | custom-call | flops 1000000000 | bytes 4000000 | tf_op jit(solution)/shard_map/second_bias/pallas_call | solution.py:317
  43.0 3.2 %collective-permute-done.2.got_ref = bf16[216,384]{1,0:T(8,128)(2,1)S(1)} collective-permute-done((bf16[216,384]{1,0:T(8,128)(2,1)}, bf16[216,384]{1,0:T(8,128)(2,1)S(1)}, u32[]{:S(2)}, u32[]{:S(2)}) %collective-permute-start.2) | collective-permute-done | bytes 165920 | tf_op jit(solution)/shard_map/ppermute | solution.py:302
  46.2 0.0 copy-start
  46.2 0.7 copy-done
  46.9 6.0 %second_block.1 = (f32[144,384]{1,0:T(8,128)}, bf16[144,384]{1,0:T(8,128)(2,1)}) custom-call(bf16[216,384]{1,0:T(8,128)(2,1)} %get-tuple-element.18.own_ref, bf16[216,384]{1,0:T(8,128)(2,1)} %copy-done, bf16[2,384,1152]{2,1,0:T(8,128)(2,1)} %qkv_w.5, f32[2,1152]{1,0:T(2,128)} %qkv_b.5, bf16[2,384,384]{2,1,0:T(8,128)(2,1)} %proj_w.5, f32[2,384]{1,0:T(2,128)} %proj_b.5, ...), custom_call_target="tpu_custom_call" | custom-call | flops 1000000000 | bytes 4000000 | tf_op jit(solution)/shard_map/second_block/pallas_call | solution.py:317
  52.9 1.9 %collective-permute-start.3 = (bf16[144,384]{1,0:T(8,128)(2,1)}, bf16[144,384]{1,0:T(8,128)(2,1)S(1)}, u32[]{:S(2)}, u32[]{:S(2)}) collective-permute-start(bf16[144,384]{1,0:T(8,128)(2,1)} %get-tuple-element.22), channel_id=1, source_target_pairs={{480,0},{0,32},{32,64},{64,96},{96,128},{128,160},{160,192},{192,2... | collective-permute-start | bytes 331784 | tf_op jit(solution)/shard_map/ppermute | solution.py:302
  54.8 16.8 %collective-permute-done.3.got_ref = bf16[144,384]{1,0:T(8,128)(2,1)S(1)} collective-permute-done((bf16[144,384]{1,0:T(8,128)(2,1)}, bf16[144,384]{1,0:T(8,128)(2,1)S(1)}, u32[]{:S(2)}, u32[]{:S(2)}) %collective-permute-start.3) | collective-permute-done | bytes 110624 | tf_op jit(solution)/shard_map/ppermute | solution.py:302
  71.6 0.0 copy-start.3
  71.6 0.6 copy-done.3
  72.3 2.0 %final_sum.1 = f32[144,2,384]{2,1,0:T(2,128)} custom-call(f32[288,384]{1,0:T(8,128)} %get-tuple-element.15.first_ref, f32[144,384]{1,0:T(8,128)} %get-tuple-element.21.keep_ref, bf16[144,384]{1,0:T(8,128)(2,1)} %copy-done.3), custom_call_target="tpu_custom_call" | custom-call | flops 1000000000 | bytes 4000000 | tf_op jit(solution)/shard_map/final_sum/pallas_call | solution.py:317
Async XLA Ops:
  1.4 19.3 %collective-permute-start = (bf16[12,6,2,384]{3,2,1,0:T(2,128)(2,1)S(1)}, bf16[12,6,2,384]{3,2,1,0:T(2,128)(2,1)S(1)}, u32[]{:S(2)}, u32[]{:S(2)}) collective-permute-start(bf16[12,6,2,384]{3,2,1,0:T(2,128)(2,1)S(1)} %get-tuple-element.24), channel_id=1, source_target_pairs={{0,1},{1,0},{2,3},{3,2},{4,5},{5,4},{6,7},{7,6},{8,9},{9,8},{10,11... | collective-permute-start | bytes 331784 | tf_op jit(solution)/shard_map/ppermute | solution.py:297
  8.8 12.0 %collective-permute-start.1 = (bf16[12,6,2,384]{3,2,1,0:T(2,128)(2,1)S(1)}, bf16[12,6,2,384]{3,2,1,0:T(2,128)(2,1)S(1)}, u32[]{:S(2)}, u32[]{:S(2)}) collective-permute-start(bf16[12,6,2,384]{3,2,1,0:T(2,128)(2,1)S(1)} %get-tuple-element.23), channel_id=1, source_target_pairs={{0,31},{1,2},{2,1},{3,4},{4,3},{5,6},{6,5},{7,8},{8,7},{9,10},{10,... | collective-permute-start | bytes 331784 | tf_op jit(solution)/shard_map/ppermute | solution.py:297
  20.7 0.6 copy-start.1
  20.7 0.7 copy-start.2
  27.1 19.2 %collective-permute-start.2 = (bf16[216,384]{1,0:T(8,128)(2,1)}, bf16[216,384]{1,0:T(8,128)(2,1)S(1)}, u32[]{:S(2)}, u32[]{:S(2)}) collective-permute-start(bf16[216,384]{1,0:T(8,128)(2,1)} %get-tuple-element.19), channel_id=1, source_target_pairs={{32,0},{64,32},{96,64},{128,96},{160,128},{192,160},{224,192},{256... | collective-permute-start | bytes 497672 | tf_op jit(solution)/shard_map/ppermute | solution.py:302
  46.2 0.7 copy-start
  52.9 18.7 %collective-permute-start.3 = (bf16[144,384]{1,0:T(8,128)(2,1)}, bf16[144,384]{1,0:T(8,128)(2,1)S(1)}, u32[]{:S(2)}, u32[]{:S(2)}) collective-permute-start(bf16[144,384]{1,0:T(8,128)(2,1)} %get-tuple-element.22), channel_id=1, source_target_pairs={{480,0},{0,32},{32,64},{64,96},{96,128},{128,160},{160,192},{192,2... | collective-permute-start | bytes 331784 | tf_op jit(solution)/shard_map/ppermute | solution.py:302
  71.6 0.6 copy-start.3
where the time goes:
time: 74.6 us; the launch traced here: 74.3 us
  Pallas kernels  26.5 us (36%)
  starting transfers between devices  23.7 us (32%)
  waiting for transfers between devices  20.1 us (27%)
  local copies, waits for them, and re-layouts  1.97 us (3%)
  other arithmetic  1.95 us (3%)
    pallas_call x6, Pallas kernels, run(): pl.pallas_call(kernel, grid=(1,), out_shape=[jax.ShapeDtypeStruct(*out) f...  26.5 us
    ppermute x2, waiting for transfers between devices, passed_along(): lax.ppermute(block, axis, [((i - distance) % count, i) for i in range(cou...  20.1 us
    ppermute x2, starting transfers between devices, passed_along(): lax.ppermute(block, axis, [((i - distance) % count, i) for i in range(cou...  14.3 us
    ppermute x2, starting transfers between devices, exchanged(): return lax.ppermute(block, 'lon', [(i, partner[i]) for i in range(count)])  9.31 us
    unnamed x8, local copies, waits for them, and re-layouts  1.97 us
  transfers between devices with their start and end apart: 4, of which 2 were waited for; matrix products, arithmetic and copies ran while one was open for 1% of the time, Pallas kernels for 17%

commit v1 on v0

--- a/solution.py
+++ b/solution.py
@@ -23,6 +23,7 @@
 LINE = WH * SPAN
 LOG2E = float(np.log2(np.e))
 VMEM_LIMIT = 60 * 1024 * 1024
+VMEM_SHARED = 40 * 1024 * 1024
 
 
 def grid_of(*sizes):
@@ -225,13 +226,13 @@
 
 
 def edge_kernel(
-    heads, place_ref, second_ref, near_ref, wrap_ref, gain_ref, offset_ref, qkv_w, qkv_b, proj_w,
+    heads, second_ref, near_ref, wrap_ref, gain_ref, offset_ref, qkv_w, qkv_b, proj_w,
     proj_b, bias_ref, side_ref, strip_ref, edge_ref, send_ref, keep_ref, core_ref,
 ):
     width = second_ref.shape[1]
     near = near_ref[...].astype(jnp.float32).reshape(TOKENS, width)
     wrap = wrap_ref[...].astype(jnp.float32).reshape(TOKENS, width)
-    odd = place_ref[1] == 1
+    odd = lax.rem(lax.axis_index("lon"), 2) == 1
     left = exact(side_ref[...], jnp.where(odd, near, wrap).astype(jnp.bfloat16))
     right = exact(side_ref[...], jnp.where(odd, wrap, near).astype(jnp.bfloat16))
     tokens = normalized(jnp.concatenate([left, right], axis=0), gain_ref[0:1], offset_ref[0:1])
@@ -251,10 +252,12 @@
     keep_ref[...] = strip[half:].astype(jnp.bfloat16)
 
 
-def bias_kernel(heads, flag_ref, table_ref, lanes_ref, rows_ref, out_ref):
+def bias_kernel(heads, table_ref, lanes_ref, rows_ref, out_ref):
     upper = lax.broadcasted_iota(jnp.int32, (TOKENS, TOKENS), 0) < CELLS
     left = lax.broadcasted_iota(jnp.int32, (TOKENS, TOKENS), 1) < CELLS
-    barred = jnp.where(upper != left, flag_ref[0] * -1000000000.0, 0.0)
+    last = lax.axis_index("lat") == lax.axis_size("lat") - 1
+    flag = jnp.where(last, 1.0, 0.0)
+    barred = jnp.where(upper != left, flag * -1000000000.0, 0.0)
     for head, dense in dense_groups(table_ref[...], lanes_ref[...], rows_ref[...], heads):
         out_ref[head] = (dense + barred) * LOG2E
 
@@ -302,8 +305,6 @@
     return lax.ppermute(block, axis, [((i - distance) % count, i) for i in range(count)])
 
 
-VMEM = pl.BlockSpec(memory_space=pltpu.VMEM)
-SMEM = pl.BlockSpec(memory_space=pltpu.SMEM)
 WHOLE = lambda shape: pl.BlockSpec(shape, lambda i: (0,) * len(shape))
 
 
@@ -312,7 +313,7 @@
     return pl.BlockSpec((None, *size), lambda i: (which,) + (0,) * len(size))
 
 
-def run(kernel, name, operands, specs, outs, scratch=(), flops=10**9):
+def run(kernel, name, operands, specs, outs, scratch=(), limit=VMEM_LIMIT):
     specs = [WHOLE(x.shape) if s is None else s for x, s in zip(operands, specs, strict=True)]
     return pl.pallas_call(
         kernel,
@@ -321,8 +322,8 @@
         in_specs=specs,
         out_specs=[WHOLE(shape) for shape, _ in outs],
         scratch_shapes=list(scratch),
-        compiler_params=pltpu.CompilerParams(vmem_limit_bytes=VMEM_LIMIT),
-        cost_estimate=pl.CostEstimate(flops=flops, bytes_accessed=4000000, transcendentals=0),
+        compiler_params=pltpu.CompilerParams(vmem_limit_bytes=limit),
+        cost_estimate=pl.CostEstimate(flops=10**9, bytes_accessed=4000000, transcendentals=0),
         name=name,
     )(*operands)
 
@@ -333,14 +334,11 @@
     depth, lat_rows, lon_cols, width = field.shape
     heads = earth_bias.shape[2]
     f32, bf16 = jnp.float32, jnp.bfloat16
-    lat, lon = lax.axis_index("lat"), lax.axis_index("lon")
-    place = jnp.stack([lat % 2, lon % 2]).astype(jnp.int32)
-    last = (lat == lax.axis_size("lat") - 1).astype(f32).reshape(1)
     native = jnp.transpose(field, (1, 2, 0, 3))
     raw = jnp.transpose(earth_bias[:, 0], (1, 0, 2))
 
     halves = native.astype(bf16)
-    odd = place[1] == 1
+    odd = lax.axis_index("lon") % 2 == 1
     to_wrap = jnp.where(odd, halves[:, WW:], halves[:, :WW])
     to_near = jnp.where(odd, halves[:, :WW], halves[:, WW:])
     wrap = exchanged(to_wrap, False)
@@ -374,23 +372,25 @@
         functools.partial(edge_kernel, heads),
         "first_block_edges",
         (
-            place, second, near.reshape(cells // 2, depth, width),
+            second, near.reshape(cells // 2, depth, width),
             wrap.reshape(cells // 2, depth, width), norm_gain, norm_bias, qkv_weight, qkv_bias,
             proj_weight, proj_bias, bias0, const(native_to_windows(1)),
             const(strip_from_native(lon_cols)), const(strip_from_sides(lon_cols)),
         ),
-        (SMEM, None, None, None, None, None, chosen(qkv_weight, 0), None, chosen(proj_weight, 0))
+        (None, None, None, None, None, chosen(qkv_weight, 0), None, chosen(proj_weight, 0))
         + (None,) * 5,
         [((strip, width), bf16), ((strip, width), bf16)],
         [pltpu.VMEM((2 * TOKENS, width), f32)],
+        limit=VMEM_SHARED,
     )
     from_above = passed_along(send, "lat", -1)
     (bias1,) = run(
         functools.partial(bias_kernel, heads),
         "second_bias",
-        (last, table1, lanes, const(full_rows())),
-        (SMEM, None, None, None),
+        (table1, lanes, const(full_rows())),
+        (None, None, None),
         [((heads, TOKENS, TOKENS), f32)],
+        limit=VMEM_SHARED,
     )
     kept, leaving = run(
         functools.partial(second_kernel, heads),
@@ -402,6 +402,7 @@
         (None, None, chosen(qkv_weight, 1), None, chosen(proj_weight, 1)) + (None,) * 3,
         [((TOKENS, width), f32), ((TOKENS, width), bf16)],
         [pltpu.VMEM((3, TOKENS, width), f32)],
+        limit=VMEM_SHARED,
     )
     from_below = passed_along(leaving, "lat", 1)
     (mixed,) = run(
@@ -410,6 +411,7 @@
         (first, kept, from_below),
         (None,) * 3,
         [((cells, depth, width), f32)],
+        limit=VMEM_SHARED,
     )
     return jnp.transpose(mixed.reshape(lat_rows, lon_cols, depth, width), (2, 0, 1, 3))
 

time: 74.6 us -> 67.8 us (0.909)
  Pallas kernels: 26.5 us -> 17.6 us
  waiting for transfers between devices: 20.1 us -> 22.1 us
    pallas_call x6, Pallas kernels: 26.5 us -> 17.6 us  [run(): pl.pallas_call(kernel, grid=(1,), out_shape=[jax.ShapeDtypeStruct(*out) f...]
    ppermute x2, waiting for transfers between devices: 20.1 us -> 22.1 us  [passed_along(): lax.ppermute(block, axis, [((i - distance) % count, i) for i in range(cou...]
    unnamed x8 -> x32, local copies, waits for them, and re-layouts: 1.97 us -> 2.47 us
  transfers between devices with their start and end apart: 4 -> 4, of which waited for: 2 -> 2; matrix products, arithmetic and copies ran while one was open for 1% -> 0% of each run, Pallas kernels for 17% -> 15%
where the time goes in v1:
time: 67.8 us; the launch traced here: 67.5 us
  starting transfers between devices  23.7 us (35%)
  waiting for transfers between devices  22.1 us (33%)
  Pallas kernels  17.6 us (26%)
  local copies, waits for them, and re-layouts  2.47 us (4%)
  other arithmetic  1.34 us (2%)
    ppermute x2, waiting for transfers between devices, passed_along(): lax.ppermute(block, axis, [((i - distance) % count, i) for i in range(cou...  22.1 us
    pallas_call x6, Pallas kernels, run(): pl.pallas_call(kernel, grid=(1,), out_shape=[jax.ShapeDtypeStruct(*out) f...  17.6 us
    ppermute x2, starting transfers between devices, passed_along(): lax.ppermute(block, axis, [((i - distance) % count, i) for i in range(cou...  14.4 us
    ppermute x2, starting transfers between devices, exchanged(): return lax.ppermute(block, 'lon', [(i, partner[i]) for i in range(count)])  9.31 us
    unnamed x32, local copies, waits for them, and re-layouts  2.47 us
  transfers between devices with their start and end apart: 4, of which 2 were waited for; matrix products, arithmetic and copies ran while one was open for 0% of the time, Pallas kernels for 15%

profile of v1, /device:TPU:32, one launch (start us, length us, event | category | flops | bytes accessed | tf_op | source)
XLA Modules:
  0.0 67.5 jit_solution(8063743429278668779)
XLA Ops:
  0.0 1.2 %bitcast_convert_fusion = bf16[12,12,2,384]{3,2,1,0:T(2,128)(2,1)S(1)} fusion(f32[2,12,12,384]{3,0,2,1:T(2,128)} %param.18), kind=kLoop, calls=%fused_computation | loop fusion | flops 110592 | bytes 663552 | tf_op jit(solution)/shard_map/convert_element_type | solution.py:340
  1.2 0.2 broadcast_select_fusion
  1.4 7.4 %collective-permute-start = (bf16[12,6,2,384]{3,2,1,0:T(2,128)(2,1)S(1)}, bf16[12,6,2,384]{3,2,1,0:T(2,128)(2,1)S(1)}, u32[]{:S(2)}, u32[]{:S(2)}) collective-permute-start(bf16[12,6,2,384]{3,2,1,0:T(2,128)(2,1)S(1)} %get-tuple-element.24), channel_id=1, source_target_pairs={{0,1},{1,0},{2,3},{3,2},{4,5},{5,4},{6,7},{7,6},{8,9},{9,8},{10,11... | collective-permute-start | bytes 331784 | tf_op jit(solution)/shard_map/ppermute | solution.py:300
  8.8 1.9 %collective-permute-start.1 = (bf16[12,6,2,384]{3,2,1,0:T(2,128)(2,1)S(1)}, bf16[12,6,2,384]{3,2,1,0:T(2,128)(2,1)S(1)}, u32[]{:S(2)}, u32[]{:S(2)}) collective-permute-start(bf16[12,6,2,384]{3,2,1,0:T(2,128)(2,1)S(1)} %get-tuple-element.23), channel_id=1, source_target_pairs={{0,31},{1,2},{2,1},{3,4},{4,3},{5,6},{6,5},{7,8},{8,7},{9,10},{10,... | collective-permute-start | bytes 331784 | tf_op jit(solution)/shard_map/ppermute | solution.py:300
  10.7 2.7 %tables.1 = (bf16[288,384]{1,0:T(8,128)(2,1)}, bf16[288,384]{1,0:T(8,128)(2,1)}) custom-call(bf16[12,2,6336]{2,1,0:T(2,128)(2,1)} %bitcast.15, bf16[96,96]{1,0:T(8,128)(2,1)} %constant.37.clone.pick_ref), custom_call_target="tpu_custom_call" | custom-call | flops 1000000000 | bytes 4000000 | tf_op jit(solution)/shard_map/tables/pallas_call | solution.py:318
  13.3 0.0 copy-start
  13.3 0.0 copy-start.1
  13.3 0.0 copy-start.4
  13.3 0.0 copy-start.5
  13.4 0.0 copy-start.7
  13.4 0.0 copy-start.10
  13.4 0.0 copy-start.11
  13.4 0.0 copy-start.12
  13.4 0.0 copy-start.13
  13.4 6.9 %first_block.1 = (f32[288,384]{1,0:T(8,128)}, bf16[288,384]{1,0:T(8,128)(2,1)}, f32[12,144,144]{2,1,0:T(8,128)}) custom-call(f32[144,2,384]{2,1,0:T(2,128)} %bitcast.14, f32[2,384]{1,0:T(2,128)} %gain_ref.3, f32[2,384]{1,0:T(2,128)} %offset_ref.3, bf16[2,384,1152]{2,1,0:T(8,128)(2,1)} %qkv_w.5, f32[2,1152]{1,0:T(2,128)} %qkv_b.5, ...), custom_call_target="tpu_custom_call" | custom-call | flops 1000000000 | bytes 4000000 | tf_op jit(solution)/shard_map/first_block/pallas_call | solution.py:318
  20.3 0.0 collective-permute-done
  20.3 0.0 collective-permute-done.1
  20.3 0.0 copy-done
  20.3 0.0 copy-done.1
  20.3 0.0 copy-done.4
  20.3 0.0 copy-done.5
  20.3 0.0 copy-done.7
  20.3 0.0 copy-done.10
  20.3 0.0 copy-done.11
  20.4 0.0 copy-done.12
  20.4 0.0 copy-done.13
  20.4 0.0 copy-start.2
  20.4 1.5 %copy-done.2 = f32[12,144,144]{2,1,0:T(8,128)S(1)} copy-done((f32[12,144,144]{2,1,0:T(8,128)S(1)}, f32[12,144,144]{2,1,0:T(8,128)}, u32[]{:S(2)}) %copy-start.2) | copy-done | bytes 995352
  21.9 0.0 copy-start.6
  21.9 0.9 %copy-done.6 = bf16[288,384]{1,0:T(8,128)(2,1)S(1)} copy-done((bf16[288,384]{1,0:T(8,128)(2,1)S(1)}, bf16[288,384]{1,0:T(8,128)(2,1)}, u32[]{:S(2)}) %copy-start.6) | copy-done | bytes 221208
  22.8 0.0 copy-start.3
  22.8 0.0 copy-start.9
  22.8 0.0 copy-start.15
  22.8 2.9 %first_block_edges.1 = (bf16[216,384]{1,0:T(8,128)(2,1)S(1)}, bf16[216,384]{1,0:T(8,128)(2,1)S(1)}) custom-call(bf16[288,384]{1,0:T(8,128)(2,1)S(1)} %copy-done.6, bf16[72,2,384]{2,1,0:T(2,128)(2,1)S(1)} %bitcast.12, bf16[72,2,384]{2,1,0:T(2,128)(2,1)S(1)} %bitcast.13, f32[2,384]{1,0:T(2,128)S(1)} %copy-done.12, f32[2,384]{1,0:T(2,128)S(1)} %copy-done.13, ...), custom_call_target="tpu_custom_call" | custom-call | flops 1000000000 | bytes 4000000 | tf_op jit(solution)/shard_map/first_block_edges/pallas_call | solution.py:318
  25.7 12.4 %collective-permute-start.2 = (bf16[216,384]{1,0:T(8,128)(2,1)S(1)}, bf16[216,384]{1,0:T(8,128)(2,1)S(1)}, u32[]{:S(2)}, u32[]{:S(2)}) collective-permute-start(bf16[216,384]{1,0:T(8,128)(2,1)S(1)} %get-tuple-element.19), channel_id=1, source_target_pairs={{32,0},{64,32},{96,64},{128,96},{160,128},{192,160},{224,192},{256... | collective-permute-start | bytes 497672 | tf_op jit(solution)/shard_map/ppermute | solution.py:305
  38.2 0.0 copy-done.3
  38.2 0.0 copy-done.9
  38.2 0.0 copy-done.15
  38.2 0.0 copy-start.8
  38.2 0.9 %second_bias.1.bias_ref = f32[12,144,144]{2,1,0:T(8,128)S(1)} custom-call(bf16[288,384]{1,0:T(8,128)(2,1)S(1)} %copy-done.15, bf16[384,1536]{1,0:T(8,128)(2,1)S(1)} %copy-done.3, bf16[144,144]{1,0:T(8,128)(2,1)S(1)} %copy-done.9), custom_call_target="tpu_custom_call" | custom-call | flops 1000000000 | bytes 4000000 | tf_op jit(solution)/shard_map/second_bias/pallas_call | solution.py:318
  39.2 5.4 %collective-permute-done.2.got_ref = bf16[216,384]{1,0:T(8,128)(2,1)S(1)} collective-permute-done((bf16[216,384]{1,0:T(8,128)(2,1)S(1)}, bf16[216,384]{1,0:T(8,128)(2,1)S(1)}, u32[]{:S(2)}, u32[]{:S(2)}) %collective-permute-start.2) | collective-permute-done | bytes 165920 | tf_op jit(solution)/shard_map/ppermute | solution.py:305
  44.6 0.0 copy-done.8
  44.6 0.0 copy-start.14
  44.6 3.4 %second_block.1 = (f32[144,384]{1,0:T(8,128)S(1)}, bf16[144,384]{1,0:T(8,128)(2,1)S(1)}) custom-call(bf16[216,384]{1,0:T(8,128)(2,1)S(1)} %get-tuple-element.18.own_ref, bf16[216,384]{1,0:T(8,128)(2,1)S(1)} %collective-permute-done.2.got_ref, bf16[2,384,1152]{2,1,0:T(8,128)(2,1)S(1)} %copy-done, f32[2,1152]{1,0:T(2,128)S(1)} %copy-done.7, ...), custom_call_target="tpu_custom_call" | custom-call | flops 1000000000 | bytes 4000000 | tf_op jit(solution)/shard_map/second_block/pallas_call | solution.py:318
  48.0 1.9 %collective-permute-start.3 = (bf16[144,384]{1,0:T(8,128)(2,1)S(1)}, bf16[144,384]{1,0:T(8,128)(2,1)S(1)}, u32[]{:S(2)}, u32[]{:S(2)}) collective-permute-start(bf16[144,384]{1,0:T(8,128)(2,1)S(1)} %get-tuple-element.22), channel_id=1, source_target_pairs={{480,0},{0,32},{32,64},{64,96},{96,128},{128,160},{160,192},{192,2... | collective-permute-start | bytes 331784 | tf_op jit(solution)/shard_map/ppermute | solution.py:305
  49.9 16.7 %collective-permute-done.3.got_ref = bf16[144,384]{1,0:T(8,128)(2,1)S(1)} collective-permute-done((bf16[144,384]{1,0:T(8,128)(2,1)S(1)}, bf16[144,384]{1,0:T(8,128)(2,1)S(1)}, u32[]{:S(2)}, u32[]{:S(2)}) %collective-permute-start.3) | collective-permute-done | bytes 110624 | tf_op jit(solution)/shard_map/ppermute | solution.py:305
  66.6 0.0 copy-done.14
  66.6 0.8 %final_sum.1 = f32[144,2,384]{2,1,0:T(2,128)} custom-call(f32[288,384]{1,0:T(8,128)S(1)} %copy-done.14, f32[144,384]{1,0:T(8,128)S(1)} %get-tuple-element.21.keep_ref, bf16[144,384]{1,0:T(8,128)(2,1)S(1)} %collective-permute-done.3.got_ref), custom_call_target="tpu_custom_call" | custom-call | flops 1000000000 | bytes 4000000 | tf_op jit(solution)/shard_map/final_sum/pallas_call | solution.py:318
Async XLA Ops:
  1.4 18.9 %collective-permute-start = (bf16[12,6,2,384]{3,2,1,0:T(2,128)(2,1)S(1)}, bf16[12,6,2,384]{3,2,1,0:T(2,128)(2,1)S(1)}, u32[]{:S(2)}, u32[]{:S(2)}) collective-permute-start(bf16[12,6,2,384]{3,2,1,0:T(2,128)(2,1)S(1)} %get-tuple-element.24), channel_id=1, source_target_pairs={{0,1},{1,0},{2,3},{3,2},{4,5},{5,4},{6,7},{7,6},{8,9},{9,8},{10,11... | collective-permute-start | bytes 331784 | tf_op jit(solution)/shard_map/ppermute | solution.py:300
  8.8 11.5 %collective-permute-start.1 = (bf16[12,6,2,384]{3,2,1,0:T(2,128)(2,1)S(1)}, bf16[12,6,2,384]{3,2,1,0:T(2,128)(2,1)S(1)}, u32[]{:S(2)}, u32[]{:S(2)}) collective-permute-start(bf16[12,6,2,384]{3,2,1,0:T(2,128)(2,1)S(1)} %get-tuple-element.23), channel_id=1, source_target_pairs={{0,31},{1,2},{2,1},{3,4},{4,3},{5,6},{6,5},{7,8},{8,7},{9,10},{10,... | collective-permute-start | bytes 331784 | tf_op jit(solution)/shard_map/ppermute | solution.py:300
  13.3 6.9 %copy-start = (bf16[2,384,1152]{2,1,0:T(8,128)(2,1)S(1)}, bf16[2,384,1152]{2,1,0:T(8,128)(2,1)}, u32[]{:S(2)}) copy-start(bf16[2,384,1152]{2,1,0:T(8,128)(2,1)} %qkv_w.5) | copy-start | bytes 5308420
  13.3 7.0 %copy-start.1 = (bf16[2,384,384]{2,1,0:T(8,128)(2,1)S(1)}, bf16[2,384,384]{2,1,0:T(8,128)(2,1)}, u32[]{:S(2)}) copy-start(bf16[2,384,384]{2,1,0:T(8,128)(2,1)} %proj_w.5) | copy-start | bytes 1769476
  13.3 7.0 %copy-start.4 = (bf16[432,288]{1,0:T(8,128)(2,1)S(1)}, bf16[432,288]{1,0:T(8,128)(2,1)}, u32[]{:S(2)}) copy-start(bf16[432,288]{1,0:T(8,128)(2,1)} %constant.42.clone.strip_ref) | copy-start | bytes 746500
  13.3 7.0 %copy-start.5 = (bf16[432,144]{1,0:T(8,128)(2,1)S(1)}, bf16[432,144]{1,0:T(8,128)(2,1)}, u32[]{:S(2)}) copy-start(bf16[432,144]{1,0:T(8,128)(2,1)} %constant.43.clone.edge_ref) | copy-start | bytes 373252
  13.4 7.0 %copy-start.7 = (f32[2,1152]{1,0:T(2,128)S(1)}, f32[2,1152]{1,0:T(2,128)}, u32[]{:S(2)}) copy-start(f32[2,1152]{1,0:T(2,128)} %qkv_b.5) | copy-start | bytes 27652
  13.4 7.0 %copy-start.10 = (bf16[144,144]{1,0:T(8,128)(2,1)S(1)}, bf16[144,144]{1,0:T(8,128)(2,1)}, u32[]{:S(2)}) copy-start(bf16[144,144]{1,0:T(8,128)(2,1)} %constant.41.clone.side_ref) | copy-start | bytes 124420
  13.4 7.0 %copy-start.11 = (f32[2,384]{1,0:T(2,128)S(1)}, f32[2,384]{1,0:T(2,128)}, u32[]{:S(2)}) copy-start(f32[2,384]{1,0:T(2,128)} %proj_b.5) | copy-start | bytes 9220
  13.4 7.0 %copy-start.12 = (f32[2,384]{1,0:T(2,128)S(1)}, f32[2,384]{1,0:T(2,128)}, u32[]{:S(2)}) copy-start(f32[2,384]{1,0:T(2,128)} %gain_ref.3) | copy-start | bytes 9220
  13.4 7.0 %copy-start.13 = (f32[2,384]{1,0:T(2,128)S(1)}, f32[2,384]{1,0:T(2,128)}, u32[]{:S(2)}) copy-start(f32[2,384]{1,0:T(2,128)} %offset_ref.3) | copy-start | bytes 9220
  20.4 1.5 %copy-start.2 = (f32[12,144,144]{2,1,0:T(8,128)S(1)}, f32[12,144,144]{2,1,0:T(8,128)}, u32[]{:S(2)}) copy-start(f32[12,144,144]{2,1,0:T(8,128)} %get-tuple-element.17.bias_ref) | copy-start | bytes 2985988
  21.9 0.9 %copy-start.6 = (bf16[288,384]{1,0:T(8,128)(2,1)S(1)}, bf16[288,384]{1,0:T(8,128)(2,1)}, u32[]{:S(2)}) copy-start(bf16[288,384]{1,0:T(8,128)(2,1)} %get-tuple-element.16.second_ref) | copy-start | bytes 663556
  22.8 15.4 %copy-start.3 = (bf16[384,1536]{1,0:T(8,128)(2,1)S(1)}, bf16[384,1536]{1,0:T(8,128)(2,1)}, u32[]{:S(2)}) copy-start(bf16[384,1536]{1,0:T(8,128)(2,1)} %constant.36.clone.lanes_ref) | copy-start | bytes 3538948
  22.8 15.4 %copy-start.9 = (bf16[144,144]{1,0:T(8,128)(2,1)S(1)}, bf16[144,144]{1,0:T(8,128)(2,1)}, u32[]{:S(2)}) copy-start(bf16[144,144]{1,0:T(8,128)(2,1)} %constant.38.clone.rows_ref) | copy-start | bytes 124420
  22.8 15.4 %copy-start.15 = (bf16[288,384]{1,0:T(8,128)(2,1)S(1)}, bf16[288,384]{1,0:T(8,128)(2,1)}, u32[]{:S(2)}) copy-start(bf16[288,384]{1,0:T(8,128)(2,1)} %get-tuple-element.20.table_ref) | copy-start | bytes 663556
  25.7 18.8 %collective-permute-start.2 = (bf16[216,384]{1,0:T(8,128)(2,1)S(1)}, bf16[216,384]{1,0:T(8,128)(2,1)S(1)}, u32[]{:S(2)}, u32[]{:S(2)}) collective-permute-start(bf16[216,384]{1,0:T(8,128)(2,1)S(1)} %get-tuple-element.19), channel_id=1, source_target_pairs={{32,0},{64,32},{96,64},{128,96},{160,128},{192,160},{224,192},{256... | collective-permute-start | bytes 497672 | tf_op jit(solution)/shard_map/ppermute | solution.py:305
  38.2 6.4 %copy-start.8 = (bf16[144,144]{1,0:T(8,128)(2,1)S(1)}, bf16[144,144]{1,0:T(8,128)(2,1)}, u32[]{:S(2)}) copy-start(bf16[144,144]{1,0:T(8,128)(2,1)} %constant.44.clone.back_ref) | copy-start | bytes 124420
  44.6 22.1 %copy-start.14 = (f32[288,384]{1,0:T(8,128)S(1)}, f32[288,384]{1,0:T(8,128)}, u32[]{:S(2)}) copy-start(f32[288,384]{1,0:T(8,128)} %get-tuple-element.15.first_ref) | copy-start | bytes 1327108
  48.0 18.6 %collective-permute-start.3 = (bf16[144,384]{1,0:T(8,128)(2,1)S(1)}, bf16[144,384]{1,0:T(8,128)(2,1)S(1)}, u32[]{:S(2)}, u32[]{:S(2)}) collective-permute-start(bf16[144,384]{1,0:T(8,128)(2,1)S(1)} %get-tuple-element.22), channel_id=1, source_target_pairs={{480,0},{0,32},{32,64},{64,96},{96,128},{128,160},{160,192},{192,2... | collective-permute-start | bytes 331784 | tf_op jit(solution)/shard_map/ppermute | solution.py:305

commit v2 on v1

--- a/solution.py
+++ b/solution.py
@@ -126,7 +126,7 @@
     return jnp.concatenate([near[:, LANES:], far[:, LANES:], tail], axis=1)
 
 
-def table_kernel(raw_ref, pick_ref, first_ref, second_ref, lines):
+def roll_tables(raw_ref, pick_ref, first_ref, second_ref, lines):
     heads = raw_ref.shape[0]
     length = raw_ref.shape[2]
     tiles = -(-length // LANES)
@@ -189,9 +189,9 @@
             scores = lax.dot_general(
                 chosen, keys, (((1,), (1,)), ((), ())), preferred_element_type=jnp.float32
             )
-            scores = scores * (LOG2E * head_dim ** (-0.5)) + bias(start // head_dim + part)
+            scores = scores * head_dim ** (-0.5) + bias(start // head_dim + part).astype(jnp.float32)
             top = jnp.max(scores, axis=-1, keepdims=True)
-            weights = jnp.exp2(scores - top).astype(jnp.bfloat16)
+            weights = jnp.exp2((scores - top) * LOG2E).astype(jnp.bfloat16)
             mixed = jnp.dot(weights, values, preferred_element_type=jnp.float32)
             total = jnp.where(mine, mixed[:, :LANES] / mixed[:, LANES:], total)
         tiles.append(total)
@@ -204,11 +204,13 @@
 
 
 def first_kernel(
-    heads, field_ref, gain_ref, offset_ref, qkv_w, qkv_b, proj_w, proj_b, table_ref, lanes_ref,
-    rows_ref, order_ref, back_ref, first_ref, second_ref, bias_ref, core_ref,
+    heads, raw_ref, pick_ref, field_ref, gain_ref, offset_ref, qkv_w, qkv_b, proj_w, proj_b,
+    lanes_ref, rows_ref, order_ref, back_ref, first_ref, second_ref, bias_ref, table1_ref, core_ref,
+    lines, table_ref,
 ):
+    roll_tables(raw_ref, pick_ref, table_ref, table1_ref, lines)
     for head, dense in dense_groups(table_ref[...], lanes_ref[...], rows_ref[...], heads):
-        bias_ref[head] = dense * LOG2E
+        bias_ref[head] = dense.astype(jnp.bfloat16)
     cells, depth, width = field_ref.shape
     grid = field_ref[...].reshape(cells * depth, width)
     tokens = normalized(grid, gain_ref[0:1], offset_ref[0:1])
@@ -259,7 +261,7 @@
     flag = jnp.where(last, 1.0, 0.0)
     barred = jnp.where(upper != left, flag * -1000000000.0, 0.0)
     for head, dense in dense_groups(table_ref[...], lanes_ref[...], rows_ref[...], heads):
-        out_ref[head] = (dense + barred) * LOG2E
+        out_ref[head] = (dense + barred).astype(jnp.bfloat16)
 
 
 def second_kernel(
@@ -346,27 +348,26 @@
 
     rows = heads * WH
     lanes = const(lane_selector())
-    table0, table1 = run(
-        table_kernel,
-        "tables",
-        (raw, const(table_rows())),
-        (None, None),
-        [((2 * rows, PACKED), bf16)] * 2,
-        [pltpu.VMEM((heads, 96, PAD), f32)],
-    )
     strip = (lon_cols + WW) * Z * HALF
     cells = lat_rows * lon_cols
-    first, second, bias0 = run(
+    first, second, bias0, table1 = run(
         functools.partial(first_kernel, heads),
         "first_block",
         (
-            native.reshape(cells, depth, width), norm_gain, norm_bias, qkv_weight, qkv_bias,
-            proj_weight, proj_bias, table0, lanes, const(full_rows()),
+            raw, const(table_rows()), native.reshape(cells, depth, width), norm_gain, norm_bias, qkv_weight, qkv_bias,
+            proj_weight, proj_bias, lanes, const(full_rows()),
             const(native_to_windows(2)), const(windows_to_native(2)),
         ),
-        (None, None, None, chosen(qkv_weight, 0), None, chosen(proj_weight, 0)) + (None,) * 6,
-        [((cells * depth, width), f32), ((cells * depth, width), bf16), ((heads, TOKENS, TOKENS), f32)],
-        [pltpu.VMEM((2 * TOKENS, width), f32)],
+        (None,) * 5 + (chosen(qkv_weight, 0), None, chosen(proj_weight, 0)) + (None,) * 5,
+        [
+            ((cells * depth, width), f32), ((cells * depth, width), bf16),
+            ((heads, TOKENS, TOKENS), bf16), ((2 * rows, PACKED), bf16),
+        ],
+        [
+            pltpu.VMEM((2 * TOKENS, width), f32),
+            pltpu.VMEM((heads, 96, PAD), f32),
+            pltpu.VMEM((2 * rows, PACKED), bf16),
+        ],
     )
     send, keep = run(
         functools.partial(edge_kernel, heads),
@@ -389,7 +390,7 @@
         "second_bias",
         (table1, lanes, const(full_rows())),
         (None, None, None),
-        [((heads, TOKENS, TOKENS), f32)],
+        [((heads, TOKENS, TOKENS), bf16)],
         limit=VMEM_SHARED,
     )
     kept, leaving = run(

time: 67.8 us -> 65.6 us (0.968)
  starting transfers between devices: 23.7 us -> 31.5 us
  waiting for transfers between devices: 22.1 us -> 14.3 us
  Pallas kernels: 17.6 us -> 15.7 us
    ppermute x2, starting transfers between devices: 9.31 us -> 17.6 us  [exchanged(): return lax.ppermute(block, 'lon', [(i, partner[i]) for i in range(count)])]
    ppermute x2, waiting for transfers between devices: 22.1 us -> 14.3 us  [passed_along(): lax.ppermute(block, axis, [((i - distance) % count, i) for i in range(cou...]
    pallas_call x6 -> x5, Pallas kernels: 17.6 us -> 15.7 us  [run(): pl.pallas_call(kernel, grid=(1,), out_shape=[jax.ShapeDtypeStruct(*out) f...]
  transfers between devices with their start and end apart: 4 -> 4, of which waited for: 2 -> 2; matrix products, arithmetic and copies ran while one was open for 0% -> 0% of each run, Pallas kernels for 15% -> 13%
where the time goes in v2:
time: 65.6 us; the launch traced here: 65.3 us
  starting transfers between devices  31.5 us (48%)
  Pallas kernels  15.7 us (24%)
  waiting for transfers between devices  14.3 us (22%)
  local copies, waits for them, and re-layouts  2.18 us (3%)
  other arithmetic  1.34 us (2%)
    ppermute x2, starting transfers between devices, exchanged(): return lax.ppermute(block, 'lon', [(i, partner[i]) for i in range(count)])  17.6 us
    pallas_call x5, Pallas kernels, run(): pl.pallas_call(kernel, grid=(1,), out_shape=[jax.ShapeDtypeStruct(*out) f...  15.7 us
    ppermute x2, waiting for transfers between devices, passed_along(): lax.ppermute(block, axis, [((i - distance) % count, i) for i in range(cou...  14.3 us
    ppermute x2, starting transfers between devices, passed_along(): lax.ppermute(block, axis, [((i - distance) % count, i) for i in range(cou...  13.9 us
    unnamed x32, local copies, waits for them, and re-layouts  2.18 us
  transfers between devices with their start and end apart: 4, of which 2 were waited for; matrix products, arithmetic and copies ran while one was open for 0% of the time, Pallas kernels for 13%

profile of v2, /device:TPU:32, one launch (start us, length us, event | category | flops | bytes accessed | tf_op | source)
XLA Modules:
  0.0 65.3 jit_solution(1815774464696411450)
XLA Ops:
  0.0 1.2 %bitcast_convert_fusion = bf16[12,12,2,384]{3,2,1,0:T(2,128)(2,1)S(1)} fusion(f32[2,12,12,384]{3,0,2,1:T(2,128)} %param.18), kind=kLoop, calls=%fused_computation | loop fusion | flops 110592 | bytes 663552 | tf_op jit(solution)/shard_map/convert_element_type | solution.py:342
  1.2 0.2 broadcast_select_fusion
  1.4 3.8 %collective-permute-start.1 = (bf16[12,6,2,384]{3,2,1,0:T(2,128)(2,1)S(1)}, bf16[12,6,2,384]{3,2,1,0:T(2,128)(2,1)S(1)}, u32[]{:S(2)}, u32[]{:S(2)}) collective-permute-start(bf16[12,6,2,384]{3,2,1,0:T(2,128)(2,1)S(1)} %get-tuple-element.21), channel_id=1, source_target_pairs={{0,31},{1,2},{2,1},{3,4},{4,3},{5,6},{6,5},{7,8},{8,7},{9,10},{10,... | collective-permute-start | bytes 331784 | tf_op jit(solution)/shard_map/ppermute | solution.py:302
  5.2 13.8 %collective-permute-start = (bf16[12,6,2,384]{3,2,1,0:T(2,128)(2,1)S(1)}, bf16[12,6,2,384]{3,2,1,0:T(2,128)(2,1)S(1)}, u32[]{:S(2)}, u32[]{:S(2)}) collective-permute-start(bf16[12,6,2,384]{3,2,1,0:T(2,128)(2,1)S(1)} %get-tuple-element.22), channel_id=1, source_target_pairs={{0,1},{1,0},{2,3},{3,2},{4,5},{5,4},{6,7},{7,6},{8,9},{9,8},{10,11... | collective-permute-start | bytes 331784 | tf_op jit(solution)/shard_map/ppermute | solution.py:302
  19.0 0.0 copy-start
  19.0 0.0 copy-start.1
  19.0 0.0 copy-start.4
  19.0 0.0 copy-start.5
  19.0 0.0 copy-start.8
  19.1 0.0 copy-start.9
  19.1 0.0 copy-start.10
  19.1 0.0 copy-start.11
  19.1 0.0 copy-start.12
  19.1 7.5 %first_block.1 = (f32[288,384]{1,0:T(8,128)}, bf16[288,384]{1,0:T(8,128)(2,1)}, bf16[12,144,144]{2,1,0:T(8,128)(2,1)}, bf16[288,384]{1,0:T(8,128)(2,1)}) custom-call(bf16[12,2,6336]{2,1,0:T(2,128)(2,1)} %bitcast.15, bf16[96,96]{1,0:T(8,128)(2,1)} %constant.37.clone.pick_ref, f32[144,2,384]{2,1,0:T(2,128)} %bitcast.14, f32[2,384]{1,0:T(2,128)} %gain_ref.3, ...), custom_call_target="tpu_custom_call" | custom-call | flops 1000000000 | bytes 4000000 | tf_op jit(solution)/shard_map/first_block/pallas_call | solution.py:320
  26.6 0.0 collective-permute-done.1
  26.6 0.0 collective-permute-done
  26.6 0.0 copy-done
  26.7 0.0 copy-done.1
  26.7 0.0 copy-done.4
  26.7 0.0 copy-done.5
  26.7 0.0 copy-done.8
  26.7 0.0 copy-done.9
  26.7 0.0 copy-done.10
  26.7 0.0 copy-done.11
  26.7 0.0 copy-done.12
  26.7 0.0 copy-start.3
  26.7 1.2 %copy-done.3 = bf16[12,144,144]{2,1,0:T(8,128)(2,1)S(1)} copy-done((bf16[12,144,144]{2,1,0:T(8,128)(2,1)S(1)}, bf16[12,144,144]{2,1,0:T(8,128)(2,1)}, u32[]{:S(2)}) %copy-start.3) | copy-done | bytes 497688
  27.9 0.0 copy-start.6
  27.9 0.9 %copy-done.6 = bf16[288,384]{1,0:T(8,128)(2,1)S(1)} copy-done((bf16[288,384]{1,0:T(8,128)(2,1)S(1)}, bf16[288,384]{1,0:T(8,128)(2,1)}, u32[]{:S(2)}) %copy-start.6) | copy-done | bytes 221208
  28.8 0.0 copy-start.2
  28.8 0.0 copy-start.7
  28.8 0.0 copy-start.14
  28.8 2.9 %first_block_edges.1 = (bf16[216,384]{1,0:T(8,128)(2,1)S(1)}, bf16[216,384]{1,0:T(8,128)(2,1)S(1)}) custom-call(bf16[288,384]{1,0:T(8,128)(2,1)S(1)} %copy-done.6, bf16[72,2,384]{2,1,0:T(2,128)(2,1)S(1)} %bitcast.13, bf16[72,2,384]{2,1,0:T(2,128)(2,1)S(1)} %bitcast.12, f32[2,384]{1,0:T(2,128)S(1)} %copy-done.10, f32[2,384]{1,0:T(2,128)S(1)} %copy-done.11, ...), custom_call_target="tpu_custom_call" | custom-call | flops 1000000000 | bytes 4000000 | tf_op jit(solution)/shard_map/first_block_edges/pallas_call | solution.py:320
  31.8 9.3 %collective-permute-start.2 = (bf16[216,384]{1,0:T(8,128)(2,1)S(1)}, bf16[216,384]{1,0:T(8,128)(2,1)S(1)}, u32[]{:S(2)}, u32[]{:S(2)}) collective-permute-start(bf16[216,384]{1,0:T(8,128)(2,1)S(1)} %get-tuple-element.17), channel_id=1, source_target_pairs={{32,0},{64,32},{96,64},{128,96},{160,128},{192,160},{224,192},{256... | collective-permute-start | bytes 497672 | tf_op jit(solution)/shard_map/ppermute | solution.py:307
  41.1 0.0 copy-done.2
  41.1 0.0 copy-done.7
  41.1 0.0 copy-done.14
  41.1 0.0 copy-start.15
  41.1 0.9 %second_bias.1.bias_ref = bf16[12,144,144]{2,1,0:T(8,128)(2,1)S(1)} custom-call(bf16[288,384]{1,0:T(8,128)(2,1)S(1)} %copy-done.14, bf16[384,1536]{1,0:T(8,128)(2,1)S(1)} %copy-done.2, bf16[144,144]{1,0:T(8,128)(2,1)S(1)} %copy-done.7), custom_call_target="tpu_custom_call" | custom-call | flops 1000000000 | bytes 4000000 | tf_op jit(solution)/shard_map/second_bias/pallas_call | solution.py:320
  42.1 1.9 %collective-permute-done.2.got_ref = bf16[216,384]{1,0:T(8,128)(2,1)S(1)} collective-permute-done((bf16[216,384]{1,0:T(8,128)(2,1)S(1)}, bf16[216,384]{1,0:T(8,128)(2,1)S(1)}, u32[]{:S(2)}, u32[]{:S(2)}) %collective-permute-start.2) | collective-permute-done | bytes 165920 | tf_op jit(solution)/shard_map/ppermute | solution.py:307
  43.9 0.0 copy-done.15
  43.9 0.0 copy-start.13
  43.9 3.5 %second_block.1 = (f32[144,384]{1,0:T(8,128)S(1)}, bf16[144,384]{1,0:T(8,128)(2,1)S(1)}) custom-call(bf16[216,384]{1,0:T(8,128)(2,1)S(1)} %get-tuple-element.16.own_ref, bf16[216,384]{1,0:T(8,128)(2,1)S(1)} %collective-permute-done.2.got_ref, bf16[2,384,1152]{2,1,0:T(8,128)(2,1)S(1)} %copy-done, f32[2,1152]{1,0:T(2,128)S(1)} %copy-done.9, ...), custom_call_target="tpu_custom_call" | custom-call | flops 1000000000 | bytes 4000000 | tf_op jit(solution)/shard_map/second_block/pallas_call | solution.py:320
  47.4 4.6 %collective-permute-start.3 = (bf16[144,384]{1,0:T(8,128)(2,1)S(1)}, bf16[144,384]{1,0:T(8,128)(2,1)S(1)}, u32[]{:S(2)}, u32[]{:S(2)}) collective-permute-start(bf16[144,384]{1,0:T(8,128)(2,1)S(1)} %get-tuple-element.20), channel_id=1, source_target_pairs={{480,0},{0,32},{32,64},{64,96},{96,128},{128,160},{160,192},{192,2... | collective-permute-start | bytes 331784 | tf_op jit(solution)/shard_map/ppermute | solution.py:307
  52.0 12.5 %collective-permute-done.3.got_ref = bf16[144,384]{1,0:T(8,128)(2,1)S(1)} collective-permute-done((bf16[144,384]{1,0:T(8,128)(2,1)S(1)}, bf16[144,384]{1,0:T(8,128)(2,1)S(1)}, u32[]{:S(2)}, u32[]{:S(2)}) %collective-permute-start.3) | collective-permute-done | bytes 110624 | tf_op jit(solution)/shard_map/ppermute | solution.py:307
  64.5 0.0 copy-done.13
  64.5 0.8 %final_sum.1 = f32[144,2,384]{2,1,0:T(2,128)} custom-call(f32[288,384]{1,0:T(8,128)S(1)} %copy-done.13, f32[144,384]{1,0:T(8,128)S(1)} %get-tuple-element.19.keep_ref, bf16[144,384]{1,0:T(8,128)(2,1)S(1)} %collective-permute-done.3.got_ref), custom_call_target="tpu_custom_call" | custom-call | flops 1000000000 | bytes 4000000 | tf_op jit(solution)/shard_map/final_sum/pallas_call | solution.py:320
Async XLA Ops:
  1.4 25.3 %collective-permute-start.1 = (bf16[12,6,2,384]{3,2,1,0:T(2,128)(2,1)S(1)}, bf16[12,6,2,384]{3,2,1,0:T(2,128)(2,1)S(1)}, u32[]{:S(2)}, u32[]{:S(2)}) collective-permute-start(bf16[12,6,2,384]{3,2,1,0:T(2,128)(2,1)S(1)} %get-tuple-element.21), channel_id=1, source_target_pairs={{0,31},{1,2},{2,1},{3,4},{4,3},{5,6},{6,5},{7,8},{8,7},{9,10},{10,... | collective-permute-start | bytes 331784 | tf_op jit(solution)/shard_map/ppermute | solution.py:302
  5.2 21.4 %collective-permute-start = (bf16[12,6,2,384]{3,2,1,0:T(2,128)(2,1)S(1)}, bf16[12,6,2,384]{3,2,1,0:T(2,128)(2,1)S(1)}, u32[]{:S(2)}, u32[]{:S(2)}) collective-permute-start(bf16[12,6,2,384]{3,2,1,0:T(2,128)(2,1)S(1)} %get-tuple-element.22), channel_id=1, source_target_pairs={{0,1},{1,0},{2,3},{3,2},{4,5},{5,4},{6,7},{7,6},{8,9},{9,8},{10,11... | collective-permute-start | bytes 331784 | tf_op jit(solution)/shard_map/ppermute | solution.py:302
  19.0 7.6 %copy-start = (bf16[2,384,1152]{2,1,0:T(8,128)(2,1)S(1)}, bf16[2,384,1152]{2,1,0:T(8,128)(2,1)}, u32[]{:S(2)}) copy-start(bf16[2,384,1152]{2,1,0:T(8,128)(2,1)} %qkv_w.5) | copy-start | bytes 5308420
  19.0 7.6 %copy-start.1 = (bf16[2,384,384]{2,1,0:T(8,128)(2,1)S(1)}, bf16[2,384,384]{2,1,0:T(8,128)(2,1)}, u32[]{:S(2)}) copy-start(bf16[2,384,384]{2,1,0:T(8,128)(2,1)} %proj_w.5) | copy-start | bytes 1769476
  19.0 7.6 %copy-start.4 = (bf16[432,288]{1,0:T(8,128)(2,1)S(1)}, bf16[432,288]{1,0:T(8,128)(2,1)}, u32[]{:S(2)}) copy-start(bf16[432,288]{1,0:T(8,128)(2,1)} %constant.42.clone.strip_ref) | copy-start | bytes 746500
  19.0 7.6 %copy-start.5 = (bf16[432,144]{1,0:T(8,128)(2,1)S(1)}, bf16[432,144]{1,0:T(8,128)(2,1)}, u32[]{:S(2)}) copy-start(bf16[432,144]{1,0:T(8,128)(2,1)} %constant.43.clone.edge_ref) | copy-start | bytes 373252
  19.0 7.6 %copy-start.8 = (bf16[144,144]{1,0:T(8,128)(2,1)S(1)}, bf16[144,144]{1,0:T(8,128)(2,1)}, u32[]{:S(2)}) copy-start(bf16[144,144]{1,0:T(8,128)(2,1)} %constant.41.clone.side_ref) | copy-start | bytes 124420
  19.1 7.6 %copy-start.9 = (f32[2,1152]{1,0:T(2,128)S(1)}, f32[2,1152]{1,0:T(2,128)}, u32[]{:S(2)}) copy-start(f32[2,1152]{1,0:T(2,128)} %qkv_b.5) | copy-start | bytes 27652
  19.1 7.6 %copy-start.10 = (f32[2,384]{1,0:T(2,128)S(1)}, f32[2,384]{1,0:T(2,128)}, u32[]{:S(2)}) copy-start(f32[2,384]{1,0:T(2,128)} %gain_ref.3) | copy-start | bytes 9220
  19.1 7.6 %copy-start.11 = (f32[2,384]{1,0:T(2,128)S(1)}, f32[2,384]{1,0:T(2,128)}, u32[]{:S(2)}) copy-start(f32[2,384]{1,0:T(2,128)} %offset_ref.3) | copy-start | bytes 9220
  19.1 7.6 %copy-start.12 = (f32[2,384]{1,0:T(2,128)S(1)}, f32[2,384]{1,0:T(2,128)}, u32[]{:S(2)}) copy-start(f32[2,384]{1,0:T(2,128)} %proj_b.5) | copy-start | bytes 9220
  26.7 1.2 %copy-start.3 = (bf16[12,144,144]{2,1,0:T(8,128)(2,1)S(1)}, bf16[12,144,144]{2,1,0:T(8,128)(2,1)}, u32[]{:S(2)}) copy-start(bf16[12,144,144]{2,1,0:T(8,128)(2,1)} %get-tuple-element.15.bias_ref) | copy-start | bytes 1492996
  27.9 0.9 %copy-start.6 = (bf16[288,384]{1,0:T(8,128)(2,1)S(1)}, bf16[288,384]{1,0:T(8,128)(2,1)}, u32[]{:S(2)}) copy-start(bf16[288,384]{1,0:T(8,128)(2,1)} %get-tuple-element.14.second_ref) | copy-start | bytes 663556
  28.8 12.2 %copy-start.2 = (bf16[384,1536]{1,0:T(8,128)(2,1)S(1)}, bf16[384,1536]{1,0:T(8,128)(2,1)}, u32[]{:S(2)}) copy-start(bf16[384,1536]{1,0:T(8,128)(2,1)} %constant.36.clone.lanes_ref) | copy-start | bytes 3538948
  28.8 12.3 %copy-start.7 = (bf16[144,144]{1,0:T(8,128)(2,1)S(1)}, bf16[144,144]{1,0:T(8,128)(2,1)}, u32[]{:S(2)}) copy-start(bf16[144,144]{1,0:T(8,128)(2,1)} %constant.38.clone.rows_ref) | copy-start | bytes 124420
  28.8 12.3 %copy-start.14 = (bf16[288,384]{1,0:T(8,128)(2,1)S(1)}, bf16[288,384]{1,0:T(8,128)(2,1)}, u32[]{:S(2)}) copy-start(bf16[288,384]{1,0:T(8,128)(2,1)} %get-tuple-element.18.table_ref) | copy-start | bytes 663556
  31.8 12.1 %collective-permute-start.2 = (bf16[216,384]{1,0:T(8,128)(2,1)S(1)}, bf16[216,384]{1,0:T(8,128)(2,1)S(1)}, u32[]{:S(2)}, u32[]{:S(2)}) collective-permute-start(bf16[216,384]{1,0:T(8,128)(2,1)S(1)} %get-tuple-element.17), channel_id=1, source_target_pairs={{32,0},{64,32},{96,64},{128,96},{160,128},{192,160},{224,192},{256... | collective-permute-start | bytes 497672 | tf_op jit(solution)/shard_map/ppermute | solution.py:307
  41.1 2.8 %copy-start.15 = (bf16[144,144]{1,0:T(8,128)(2,1)S(1)}, bf16[144,144]{1,0:T(8,128)(2,1)}, u32[]{:S(2)}) copy-start(bf16[144,144]{1,0:T(8,128)(2,1)} %constant.44.clone.back_ref) | copy-start | bytes 124420
  43.9 20.6 %copy-start.13 = (f32[288,384]{1,0:T(8,128)S(1)}, f32[288,384]{1,0:T(8,128)}, u32[]{:S(2)}) copy-start(f32[288,384]{1,0:T(8,128)} %get-tuple-element.13.first_ref) | copy-start | bytes 1327108
  47.4 17.1 %collective-permute-start.3 = (bf16[144,384]{1,0:T(8,128)(2,1)S(1)}, bf16[144,384]{1,0:T(8,128)(2,1)S(1)}, u32[]{:S(2)}, u32[]{:S(2)}) collective-permute-start(bf16[144,384]{1,0:T(8,128)(2,1)S(1)} %get-tuple-element.20), channel_id=1, source_target_pairs={{480,0},{0,32},{32,64},{64,96},{96,128},{128,160},{160,192},{192,2... | collective-permute-start | bytes 331784 | tf_op jit(solution)/shard_map/ppermute | solution.py:307

commit v3 on v2

--- a/solution.py
+++ b/solution.py
@@ -230,7 +230,12 @@
 def edge_kernel(
     heads, second_ref, near_ref, wrap_ref, gain_ref, offset_ref, qkv_w, qkv_b, proj_w,
     proj_b, bias_ref, side_ref, strip_ref, edge_ref, send_ref, keep_ref, core_ref,
+    bias_here, second_here, bias_sem, second_sem,
 ):
+    bias_copy = pltpu.make_async_copy(bias_ref, bias_here, bias_sem)
+    second_copy = pltpu.make_async_copy(second_ref, second_here, second_sem)
+    bias_copy.start()
+    second_copy.start()
     width = second_ref.shape[1]
     near = near_ref[...].astype(jnp.float32).reshape(TOKENS, width)
     wrap = wrap_ref[...].astype(jnp.float32).reshape(TOKENS, width)
@@ -240,15 +245,17 @@
     tokens = normalized(jnp.concatenate([left, right], axis=0), gain_ref[0:1], offset_ref[0:1])
     packed = jnp.dot(tokens, qkv_w[...], preferred_element_type=jnp.float32) + qkv_b[0:1]
     packed = packed.astype(jnp.bfloat16)
+    bias_copy.wait()
     for window in range(2):
         at = slice(window * TOKENS, (window + 1) * TOKENS)
-        core_ref[at] = attend(packed[at], bias_ref.__getitem__, heads)
+        core_ref[at] = attend(packed[at], bias_here.__getitem__, heads)
     inner = inner_columns(TOKENS, width)
     core = jnp.where(inner, core_ref[TOKENS:], core_ref[:TOKENS]).astype(jnp.bfloat16)
     result = jnp.dot(core, proj_w[...], preferred_element_type=jnp.float32) + proj_b[0:1]
     edge = jnp.where(inner, right, left) + result
     edge = normalized(edge, gain_ref[1:2], offset_ref[1:2])
-    strip = exact(strip_ref[...], second_ref[...]) + exact(edge_ref[...], edge)
+    second_copy.wait()
+    strip = exact(strip_ref[...], second_here[...]) + exact(edge_ref[...], edge)
     half = strip.shape[0] // 2
     send_ref[...] = strip[:half].astype(jnp.bfloat16)
     keep_ref[...] = strip[half:].astype(jnp.bfloat16)
@@ -307,6 +314,7 @@
     return lax.ppermute(block, axis, [((i - distance) % count, i) for i in range(count)])
 
 
+ANY = pl.BlockSpec(memory_space=pl.ANY)
 WHOLE = lambda shape: pl.BlockSpec(shape, lambda i: (0,) * len(shape))
 
 
@@ -378,10 +386,16 @@
             proj_weight, proj_bias, bias0, const(native_to_windows(1)),
             const(strip_from_native(lon_cols)), const(strip_from_sides(lon_cols)),
         ),
-        (None, None, None, None, None, chosen(qkv_weight, 0), None, chosen(proj_weight, 0))
-        + (None,) * 5,
+        (ANY, None, None, None, None, chosen(qkv_weight, 0), None, chosen(proj_weight, 0), None, ANY)
+        + (None,) * 3,
         [((strip, width), bf16), ((strip, width), bf16)],
-        [pltpu.VMEM((2 * TOKENS, width), f32)],
+        [
+            pltpu.VMEM((2 * TOKENS, width), f32),
+            pltpu.VMEM((heads, TOKENS, TOKENS), bf16),
+            pltpu.VMEM((cells * depth, width), bf16),
+            pltpu.SemaphoreType.DMA,
+            pltpu.SemaphoreType.DMA,
+        ],
         limit=VMEM_SHARED,
     )
     from_above = passed_along(send, "lat", -1)

time: 65.6 us -> 66.3 us (1.011)
  Pallas kernels: 15.7 us -> 16.4 us
where the time goes in v3:
time: 66.3 us; the launch traced here: 66 us
  starting transfers between devices  31.5 us (48%)
  Pallas kernels  16.4 us (25%)
  waiting for transfers between devices  14.3 us (22%)
  local copies, waits for them, and re-layouts  2.18 us (3%)
  other arithmetic  1.34 us (2%)
    ppermute x2, starting transfers between devices, exchanged(): return lax.ppermute(block, 'lon', [(i, partner[i]) for i in range(count)])  17.6 us
    pallas_call x5, Pallas kernels, run(): pl.pallas_call(kernel, grid=(1,), out_shape=[jax.ShapeDtypeStruct(*out) f...  16.4 us
    ppermute x2, waiting for transfers between devices, passed_along(): lax.ppermute(block, axis, [((i - distance) % count, i) for i in range(cou...  14.3 us
    ppermute x2, starting transfers between devices, passed_along(): lax.ppermute(block, axis, [((i - distance) % count, i) for i in range(cou...  13.9 us
    unnamed x32, local copies, waits for them, and re-layouts  2.18 us
  transfers between devices with their start and end apart: 4, of which 2 were waited for; matrix products, arithmetic and copies ran while one was open for 0% of the time, Pallas kernels for 13%

profile of v3, /device:TPU:32, one launch (start us, length us, event | category | flops | bytes accessed | tf_op | source)
XLA Modules:
  0.0 66.0 jit_solution(13255573124863814083)
XLA Ops:
  0.0 1.2 %bitcast_convert_fusion = bf16[12,12,2,384]{3,2,1,0:T(2,128)(2,1)S(1)} fusion(f32[2,12,12,384]{3,0,2,1:T(2,128)} %param.18), kind=kLoop, calls=%fused_computation | loop fusion | flops 110592 | bytes 663552 | tf_op jit(solution)/shard_map/convert_element_type | solution.py:350
  1.2 0.2 broadcast_select_fusion
  1.4 3.8 %collective-permute-start.1 = (bf16[12,6,2,384]{3,2,1,0:T(2,128)(2,1)S(1)}, bf16[12,6,2,384]{3,2,1,0:T(2,128)(2,1)S(1)}, u32[]{:S(2)}, u32[]{:S(2)}) collective-permute-start(bf16[12,6,2,384]{3,2,1,0:T(2,128)(2,1)S(1)} %get-tuple-element.21), channel_id=1, source_target_pairs={{0,31},{1,2},{2,1},{3,4},{4,3},{5,6},{6,5},{7,8},{8,7},{9,10},{10,... | collective-permute-start | bytes 331784 | tf_op jit(solution)/shard_map/ppermute | solution.py:309
  5.2 13.8 %collective-permute-start = (bf16[12,6,2,384]{3,2,1,0:T(2,128)(2,1)S(1)}, bf16[12,6,2,384]{3,2,1,0:T(2,128)(2,1)S(1)}, u32[]{:S(2)}, u32[]{:S(2)}) collective-permute-start(bf16[12,6,2,384]{3,2,1,0:T(2,128)(2,1)S(1)} %get-tuple-element.22), channel_id=1, source_target_pairs={{0,1},{1,0},{2,3},{3,2},{4,5},{5,4},{6,7},{7,6},{8,9},{9,8},{10,11... | collective-permute-start | bytes 331784 | tf_op jit(solution)/shard_map/ppermute | solution.py:309
  19.0 0.0 copy-start
  19.0 0.0 copy-start.1
  19.0 0.0 copy-start.4
  19.0 0.0 copy-start.5
  19.0 0.0 copy-start.8
  19.1 0.0 copy-start.9
  19.1 0.0 copy-start.10
  19.1 0.0 copy-start.11
  19.1 0.0 copy-start.12
  19.1 7.5 %first_block.1 = (f32[288,384]{1,0:T(8,128)}, bf16[288,384]{1,0:T(8,128)(2,1)}, bf16[12,144,144]{2,1,0:T(8,128)(2,1)}, bf16[288,384]{1,0:T(8,128)(2,1)}) custom-call(bf16[12,2,6336]{2,1,0:T(2,128)(2,1)} %bitcast.15, bf16[96,96]{1,0:T(8,128)(2,1)} %constant.37.clone.pick_ref, f32[144,2,384]{2,1,0:T(2,128)} %bitcast.14, f32[2,384]{1,0:T(2,128)} %gain_ref.3, ...), custom_call_target="tpu_custom_call" | custom-call | flops 1000000000 | bytes 4000000 | tf_op jit(solution)/shard_map/first_block/pallas_call | solution.py:328
  26.6 0.0 collective-permute-done.1
  26.6 0.0 collective-permute-done
  26.6 0.0 copy-done
  26.7 0.0 copy-done.1
  26.7 0.0 copy-done.4
  26.7 0.0 copy-done.5
  26.7 0.0 copy-done.8
  26.7 0.0 copy-done.9
  26.7 0.0 copy-done.10
  26.7 0.0 copy-done.11
  26.7 0.0 copy-done.12
  26.7 0.0 copy-start.3
  26.7 1.2 %copy-done.3 = bf16[12,144,144]{2,1,0:T(8,128)(2,1)S(1)} copy-done((bf16[12,144,144]{2,1,0:T(8,128)(2,1)S(1)}, bf16[12,144,144]{2,1,0:T(8,128)(2,1)}, u32[]{:S(2)}) %copy-start.3) | copy-done | bytes 497688
  27.9 0.0 copy-start.6
  27.9 0.9 %copy-done.6 = bf16[288,384]{1,0:T(8,128)(2,1)S(1)} copy-done((bf16[288,384]{1,0:T(8,128)(2,1)S(1)}, bf16[288,384]{1,0:T(8,128)(2,1)}, u32[]{:S(2)}) %copy-start.6) | copy-done | bytes 221208
  28.8 0.0 copy-start.2
  28.8 0.0 copy-start.7
  28.8 0.0 copy-start.14
  28.8 3.6 %first_block_edges.1 = (bf16[216,384]{1,0:T(8,128)(2,1)S(1)}, bf16[216,384]{1,0:T(8,128)(2,1)S(1)}) custom-call(bf16[288,384]{1,0:T(8,128)(2,1)S(1)} %copy-done.6, bf16[72,2,384]{2,1,0:T(2,128)(2,1)S(1)} %bitcast.13, bf16[72,2,384]{2,1,0:T(2,128)(2,1)S(1)} %bitcast.12, f32[2,384]{1,0:T(2,128)S(1)} %copy-done.10, f32[2,384]{1,0:T(2,128)S(1)} %copy-done.11, ...), custom_call_target="tpu_custom_call" | custom-call | flops 1000000000 | bytes 4000000 | tf_op jit(solution)/shard_map/first_block_edges/pallas_call | solution.py:328
  32.4 9.3 %collective-permute-start.2 = (bf16[216,384]{1,0:T(8,128)(2,1)S(1)}, bf16[216,384]{1,0:T(8,128)(2,1)S(1)}, u32[]{:S(2)}, u32[]{:S(2)}) collective-permute-start(bf16[216,384]{1,0:T(8,128)(2,1)S(1)} %get-tuple-element.17), channel_id=1, source_target_pairs={{32,0},{64,32},{96,64},{128,96},{160,128},{192,160},{224,192},{256... | collective-permute-start | bytes 497672 | tf_op jit(solution)/shard_map/ppermute | solution.py:314
  41.7 0.0 copy-done.2
  41.7 0.0 copy-done.7
  41.8 0.0 copy-done.14
  41.8 0.0 copy-start.15
  41.8 0.9 %second_bias.1.bias_ref = bf16[12,144,144]{2,1,0:T(8,128)(2,1)S(1)} custom-call(bf16[288,384]{1,0:T(8,128)(2,1)S(1)} %copy-done.14, bf16[384,1536]{1,0:T(8,128)(2,1)S(1)} %copy-done.2, bf16[144,144]{1,0:T(8,128)(2,1)S(1)} %copy-done.7), custom_call_target="tpu_custom_call" | custom-call | flops 1000000000 | bytes 4000000 | tf_op jit(solution)/shard_map/second_bias/pallas_call | solution.py:328
  42.7 1.9 %collective-permute-done.2.got_ref = bf16[216,384]{1,0:T(8,128)(2,1)S(1)} collective-permute-done((bf16[216,384]{1,0:T(8,128)(2,1)S(1)}, bf16[216,384]{1,0:T(8,128)(2,1)S(1)}, u32[]{:S(2)}, u32[]{:S(2)}) %collective-permute-start.2) | collective-permute-done | bytes 165920 | tf_op jit(solution)/shard_map/ppermute | solution.py:314
  44.6 0.0 copy-done.15
  44.6 0.0 copy-start.13
  44.6 3.5 %second_block.1 = (f32[144,384]{1,0:T(8,128)S(1)}, bf16[144,384]{1,0:T(8,128)(2,1)S(1)}) custom-call(bf16[216,384]{1,0:T(8,128)(2,1)S(1)} %get-tuple-element.16.own_ref, bf16[216,384]{1,0:T(8,128)(2,1)S(1)} %collective-permute-done.2.got_ref, bf16[2,384,1152]{2,1,0:T(8,128)(2,1)S(1)} %copy-done, f32[2,1152]{1,0:T(2,128)S(1)} %copy-done.9, ...), custom_call_target="tpu_custom_call" | custom-call | flops 1000000000 | bytes 4000000 | tf_op jit(solution)/shard_map/second_block/pallas_call | solution.py:328
  48.1 4.6 %collective-permute-start.3 = (bf16[144,384]{1,0:T(8,128)(2,1)S(1)}, bf16[144,384]{1,0:T(8,128)(2,1)S(1)}, u32[]{:S(2)}, u32[]{:S(2)}) collective-permute-start(bf16[144,384]{1,0:T(8,128)(2,1)S(1)} %get-tuple-element.20), channel_id=1, source_target_pairs={{480,0},{0,32},{32,64},{64,96},{96,128},{128,160},{160,192},{192,2... | collective-permute-start | bytes 331784 | tf_op jit(solution)/shard_map/ppermute | solution.py:314
  52.7 12.4 %collective-permute-done.3.got_ref = bf16[144,384]{1,0:T(8,128)(2,1)S(1)} collective-permute-done((bf16[144,384]{1,0:T(8,128)(2,1)S(1)}, bf16[144,384]{1,0:T(8,128)(2,1)S(1)}, u32[]{:S(2)}, u32[]{:S(2)}) %collective-permute-start.3) | collective-permute-done | bytes 110624 | tf_op jit(solution)/shard_map/ppermute | solution.py:314
  65.1 0.0 copy-done.13
  65.1 0.8 %final_sum.1 = f32[144,2,384]{2,1,0:T(2,128)} custom-call(f32[288,384]{1,0:T(8,128)S(1)} %copy-done.13, f32[144,384]{1,0:T(8,128)S(1)} %get-tuple-element.19.keep_ref, bf16[144,384]{1,0:T(8,128)(2,1)S(1)} %collective-permute-done.3.got_ref), custom_call_target="tpu_custom_call" | custom-call | flops 1000000000 | bytes 4000000 | tf_op jit(solution)/shard_map/final_sum/pallas_call | solution.py:328
Async XLA Ops:
  1.4 25.3 %collective-permute-start.1 = (bf16[12,6,2,384]{3,2,1,0:T(2,128)(2,1)S(1)}, bf16[12,6,2,384]{3,2,1,0:T(2,128)(2,1)S(1)}, u32[]{:S(2)}, u32[]{:S(2)}) collective-permute-start(bf16[12,6,2,384]{3,2,1,0:T(2,128)(2,1)S(1)} %get-tuple-element.21), channel_id=1, source_target_pairs={{0,31},{1,2},{2,1},{3,4},{4,3},{5,6},{6,5},{7,8},{8,7},{9,10},{10,... | collective-permute-start | bytes 331784 | tf_op jit(solution)/shard_map/ppermute | solution.py:309
  5.2 21.4 %collective-permute-start = (bf16[12,6,2,384]{3,2,1,0:T(2,128)(2,1)S(1)}, bf16[12,6,2,384]{3,2,1,0:T(2,128)(2,1)S(1)}, u32[]{:S(2)}, u32[]{:S(2)}) collective-permute-start(bf16[12,6,2,384]{3,2,1,0:T(2,128)(2,1)S(1)} %get-tuple-element.22), channel_id=1, source_target_pairs={{0,1},{1,0},{2,3},{3,2},{4,5},{5,4},{6,7},{7,6},{8,9},{9,8},{10,11... | collective-permute-start | bytes 331784 | tf_op jit(solution)/shard_map/ppermute | solution.py:309
  19.0 7.6 %copy-start = (bf16[2,384,1152]{2,1,0:T(8,128)(2,1)S(1)}, bf16[2,384,1152]{2,1,0:T(8,128)(2,1)}, u32[]{:S(2)}) copy-start(bf16[2,384,1152]{2,1,0:T(8,128)(2,1)} %qkv_w.5) | copy-start | bytes 5308420
  19.0 7.6 %copy-start.1 = (bf16[2,384,384]{2,1,0:T(8,128)(2,1)S(1)}, bf16[2,384,384]{2,1,0:T(8,128)(2,1)}, u32[]{:S(2)}) copy-start(bf16[2,384,384]{2,1,0:T(8,128)(2,1)} %proj_w.5) | copy-start | bytes 1769476
  19.0 7.6 %copy-start.4 = (bf16[432,288]{1,0:T(8,128)(2,1)S(1)}, bf16[432,288]{1,0:T(8,128)(2,1)}, u32[]{:S(2)}) copy-start(bf16[432,288]{1,0:T(8,128)(2,1)} %constant.42.clone.strip_ref) | copy-start | bytes 746500
  19.0 7.6 %copy-start.5 = (bf16[432,144]{1,0:T(8,128)(2,1)S(1)}, bf16[432,144]{1,0:T(8,128)(2,1)}, u32[]{:S(2)}) copy-start(bf16[432,144]{1,0:T(8,128)(2,1)} %constant.43.clone.edge_ref) | copy-start | bytes 373252
  19.0 7.6 %copy-start.8 = (bf16[144,144]{1,0:T(8,128)(2,1)S(1)}, bf16[144,144]{1,0:T(8,128)(2,1)}, u32[]{:S(2)}) copy-start(bf16[144,144]{1,0:T(8,128)(2,1)} %constant.41.clone.side_ref) | copy-start | bytes 124420
  19.1 7.6 %copy-start.9 = (f32[2,1152]{1,0:T(2,128)S(1)}, f32[2,1152]{1,0:T(2,128)}, u32[]{:S(2)}) copy-start(f32[2,1152]{1,0:T(2,128)} %qkv_b.5) | copy-start | bytes 27652
  19.1 7.6 %copy-start.10 = (f32[2,384]{1,0:T(2,128)S(1)}, f32[2,384]{1,0:T(2,128)}, u32[]{:S(2)}) copy-start(f32[2,384]{1,0:T(2,128)} %gain_ref.3) | copy-start | bytes 9220
  19.1 7.6 %copy-start.11 = (f32[2,384]{1,0:T(2,128)S(1)}, f32[2,384]{1,0:T(2,128)}, u32[]{:S(2)}) copy-start(f32[2,384]{1,0:T(2,128)} %offset_ref.3) | copy-start | bytes 9220
  19.1 7.6 %copy-start.12 = (f32[2,384]{1,0:T(2,128)S(1)}, f32[2,384]{1,0:T(2,128)}, u32[]{:S(2)}) copy-start(f32[2,384]{1,0:T(2,128)} %proj_b.5) | copy-start | bytes 9220
  26.7 1.2 %copy-start.3 = (bf16[12,144,144]{2,1,0:T(8,128)(2,1)S(1)}, bf16[12,144,144]{2,1,0:T(8,128)(2,1)}, u32[]{:S(2)}) copy-start(bf16[12,144,144]{2,1,0:T(8,128)(2,1)} %get-tuple-element.15.bias_ref) | copy-start | bytes 1492996
  27.9 0.9 %copy-start.6 = (bf16[288,384]{1,0:T(8,128)(2,1)S(1)}, bf16[288,384]{1,0:T(8,128)(2,1)}, u32[]{:S(2)}) copy-start(bf16[288,384]{1,0:T(8,128)(2,1)} %get-tuple-element.14.second_ref) | copy-start | bytes 663556
  28.8 12.9 %copy-start.2 = (bf16[384,1536]{1,0:T(8,128)(2,1)S(1)}, bf16[384,1536]{1,0:T(8,128)(2,1)}, u32[]{:S(2)}) copy-start(bf16[384,1536]{1,0:T(8,128)(2,1)} %constant.36.clone.lanes_ref) | copy-start | bytes 3538948
  28.8 12.9 %copy-start.7 = (bf16[144,144]{1,0:T(8,128)(2,1)S(1)}, bf16[144,144]{1,0:T(8,128)(2,1)}, u32[]{:S(2)}) copy-start(bf16[144,144]{1,0:T(8,128)(2,1)} %constant.38.clone.rows_ref) | copy-start | bytes 124420
  28.8 12.9 %copy-start.14 = (bf16[288,384]{1,0:T(8,128)(2,1)S(1)}, bf16[288,384]{1,0:T(8,128)(2,1)}, u32[]{:S(2)}) copy-start(bf16[288,384]{1,0:T(8,128)(2,1)} %get-tuple-element.18.table_ref) | copy-start | bytes 663556
  32.4 12.1 %collective-permute-start.2 = (bf16[216,384]{1,0:T(8,128)(2,1)S(1)}, bf16[216,384]{1,0:T(8,128)(2,1)S(1)}, u32[]{:S(2)}, u32[]{:S(2)}) collective-permute-start(bf16[216,384]{1,0:T(8,128)(2,1)S(1)} %get-tuple-element.17), channel_id=1, source_target_pairs={{32,0},{64,32},{96,64},{128,96},{160,128},{192,160},{224,192},{256... | collective-permute-start | bytes 497672 | tf_op jit(solution)/shard_map/ppermute | solution.py:314
  41.8 2.8 %copy-start.15 = (bf16[144,144]{1,0:T(8,128)(2,1)S(1)}, bf16[144,144]{1,0:T(8,128)(2,1)}, u32[]{:S(2)}) copy-start(bf16[144,144]{1,0:T(8,128)(2,1)} %constant.44.clone.back_ref) | copy-start | bytes 124420
  44.6 20.5 %copy-start.13 = (f32[288,384]{1,0:T(8,128)S(1)}, f32[288,384]{1,0:T(8,128)}, u32[]{:S(2)}) copy-start(f32[288,384]{1,0:T(8,128)} %get-tuple-element.13.first_ref) | copy-start | bytes 1327108
  48.1 17.1 %collective-permute-start.3 = (bf16[144,384]{1,0:T(8,128)(2,1)S(1)}, bf16[144,384]{1,0:T(8,128)(2,1)S(1)}, u32[]{:S(2)}, u32[]{:S(2)}) collective-permute-start(bf16[144,384]{1,0:T(8,128)(2,1)S(1)} %get-tuple-element.20), channel_id=1, source_target_pairs={{480,0},{0,32},{32,64},{64,96},{96,128},{128,160},{160,192},{192,2... | collective-permute-start | bytes 331784 | tf_op jit(solution)/shard_map/ppermute | solution.py:314
